TPU v7x, 32 devices: a whole 2x2x4 slice. The times are simulated.
32 devices in a mesh: lat: 4 (over x, core), lon: 8 (over z, y).
Axes of the slice: x: 2, y: 2, z: 4, core: 2. Of those that a mesh axis runs over, the one named last changes fastest.
Arguments:
- tendencies: bfloat16 [3, 64, 2880, 128], P(None, 'lat', 'lon'), may hold values from -6 to 6
- bands: int32 [64], replicated, may hold values from 45 to 180
- winds: float32 [2, 64, 2880, 128], P(None, 'lat', 'lon'), may hold values from -6 to 6
- tracers: float32 [5, 64, 2880, 128], P(None, 'lat', 'lon'), may hold values from -6 to 6
Outputs:
- filtered: bfloat16 [3, 64, 2880, 128], P(None, 'lat', 'lon')
- advected: float32 [5, 64, 2880, 128], P(None, 'lat', 'lon')
All inputs are finite; a program needn't handle non-finite values.
Results may differ from a plain program's by a relative error of at most 0.0038.
Values may be sent and summed in bfloat16 or wider, within the bound.
A program may use at most 192 MiB of HBM per device.

v0:
```python
import math

import jax
import jax.numpy as jnp
from jax import lax
from jax.sharding import PartitionSpec as P

HEMI = 720


def swapped(array, axis, apart):
    return lax.ppermute(array, axis, [(i, i ^ 1 << apart) for i in range(lax.axis_size(axis))])


def extended(block, sides, width, periodic):
    for axis, dim in sides:
        count = lax.axis_size(axis)
        forward = [(i, i + 1) for i in range(count - 1)]
        if periodic:
            forward.append((count - 1, 0))
        backward = [(target, source) for source, target in forward]
        low = lax.ppermute(
            lax.slice_in_dim(block, block.shape[dim] - width, None, axis=dim), axis, forward
        )
        high = lax.ppermute(lax.slice_in_dim(block, 0, width, axis=dim), axis, backward)
        block = jnp.concatenate([low, block, high], axis=dim)
    return block


def latitude_factors(row_ids, lat_count):
    grid_row = row_ids.astype(jnp.float32) + jnp.float32(HEMI // 2 - lat_count // 2)
    centre_cos = jnp.sin(math.pi * (grid_row + 0.5) / (2.0 * HEMI))
    face_cos = jnp.sin(math.pi * grid_row / (2.0 * HEMI))
    return (centre_cos, face_cos)


def damping_rows(row_ids, lat_count):
    position = row_ids.astype(jnp.float32)
    return 0.25 + 0.5 * (position + 0.5) / (lat_count / 2.0)


def wave_tables(wave_block, lon_count):
    cell_index = jnp.arange(lon_count, dtype=jnp.int32)
    phase_index = cell_index[:, None] * wave_block[None, :] % lon_count
    phase_angle = phase_index.astype(jnp.float32) * (2.0 * math.pi / lon_count)
    return (jnp.cos(phase_angle), jnp.sin(phase_angle))


def wave_weights(wave_block, band_rows, damping, lon_count):
    half_wave = lon_count // 2
    multiplier = jnp.where(
        wave_block[None, :] <= band_rows[:, None], jnp.float32(1.0), damping[:, None]
    )
    fold_count = jnp.where((wave_block == 0) | (wave_block == half_wave), 1.0, 2.0)
    fold_count = jnp.where(wave_block > half_wave, 0.0, fold_count)
    return (multiplier - 1.0) * fold_count[None, :] / lon_count


def spectral_rows(row_data, band_rows, damping):
    lon_count = row_data.shape[2]
    block_width = 128
    block_total = lon_count // 2 // block_width + 1

    def one_block(block_number, running):
        wave_block = block_number * block_width + jnp.arange(block_width, dtype=jnp.int32)
        cos_table, sin_table = wave_tables(wave_block, lon_count)
        weights = wave_weights(wave_block, band_rows, damping, lon_count)[None, :, :, None]
        cos_part = jnp.einsum("frml,mk->frkl", row_data, cos_table, precision=lax.Precision.HIGH)
        sin_part = jnp.einsum("frml,mk->frkl", row_data, sin_table, precision=lax.Precision.HIGH)
        running = running + jnp.einsum(
            "frkl,mk->frml", cos_part * weights, cos_table, precision=lax.Precision.HIGH
        )
        return running + jnp.einsum(
            "frkl,mk->frml", sin_part * weights, sin_table, precision=lax.Precision.HIGH
        )

    return row_data + lax.fori_loop(0, block_total, one_block, jnp.zeros_like(row_data))


def polar_filter(work_rows, band_rows, damping):
    filtered_rows = spectral_rows(
        lax.all_to_all(work_rows, "lon", split_axis=3, concat_axis=2, tiled=True).astype(
            jnp.float32
        ),
        band_rows,
        damping,
    ).astype(jnp.bfloat16)
    return lax.all_to_all(filtered_rows, "lon", split_axis=2, concat_axis=3, tiled=True)


def per_device(tendencies, bands, winds, tracers):
    lat_rows = tendencies.shape[1]
    lat_devices = lax.axis_size("lat")
    lat_count = lat_devices * lat_rows
    lat_place = lax.axis_index("lat")
    polar_side = lat_place < lat_devices // 2
    half_rows = lat_rows // 2
    swap_bit = lat_devices.bit_length() - 2
    received = swapped(tendencies[:, half_rows:], "lat", swap_bit)
    work_rows = jnp.where(polar_side, tendencies[:, :half_rows], received)
    partner = jnp.bitwise_xor(lat_place, lat_devices // 2)
    offsets = jnp.arange(half_rows, dtype=jnp.int32)
    row_ids = jnp.where(
        polar_side, lat_place * lat_rows + offsets, partner * lat_rows + half_rows + offsets
    )
    filtered_rows = polar_filter(
        work_rows, jnp.take(bands, row_ids), damping_rows(row_ids, lat_count)
    )
    returned = swapped(filtered_rows, "lat", swap_bit)
    filtered = jnp.where(polar_side, jnp.concatenate([filtered_rows, returned], axis=1), tendencies)
    own_ids = lat_place * lat_rows + jnp.arange(lat_rows, dtype=jnp.int32)
    centre_cos, face_cos = latitude_factors(own_ids, lat_count)
    next_centre, face_next = latitude_factors(own_ids + 1, lat_count)
    new_winds = winds + filtered[0:2].astype(jnp.float32)
    east_courant = 0.5 * jnp.tanh(new_winds[0])
    north_courant = 0.25 * jnp.tanh(new_winds[1])
    tracer_count = tracers.shape[0]
    north_stack = jnp.concatenate([tracers, north_courant[None]], axis=0)
    lat_padded = extended(north_stack.astype(jnp.bfloat16), (("lat", 1),), 1, False).astype(
        north_stack.dtype
    )
    east_stack = jnp.concatenate([tracers, east_courant[None]], axis=0)
    lon_padded = extended(east_stack.astype(jnp.bfloat16), (("lon", 2),), 1, True).astype(
        east_stack.dtype
    )
    prior_rows = lat_padded[:tracer_count, :-2]
    next_rows = lat_padded[:tracer_count, 2:]
    next_courant = lat_padded[tracer_count, 2:]
    west_cells = lon_padded[:tracer_count, :, :-2]
    east_cells = lon_padded[:tracer_count, :, 2:]
    east_next = lon_padded[tracer_count, :, 2:]
    f_west = jnp.maximum(east_courant, 0.0) * west_cells + jnp.minimum(east_courant, 0.0) * tracers
    f_east = jnp.maximum(east_next, 0.0) * tracers + jnp.minimum(east_next, 0.0) * east_cells
    g_pole = face_cos[:, None, None] * (
        jnp.maximum(north_courant, 0.0) * prior_rows + jnp.minimum(north_courant, 0.0) * tracers
    )
    g_next = face_next[:, None, None] * (
        jnp.maximum(next_courant, 0.0) * tracers + jnp.minimum(next_courant, 0.0) * next_rows
    )
    advected = tracers - (f_east - f_west) - (g_next - g_pole) / centre_cos[:, None, None]
    return (filtered, advected)


def solution(mesh):
    return jax.shard_map(
        per_device,
        mesh=mesh,
        in_specs=(
            P(None, "lat", "lon", None),
            P(),
            P(None, "lat", "lon", None),
            P(None, "lat", "lon", None),
        ),
        out_specs=(P(None, "lat", "lon", None), P(None, "lat", "lon", None)),
        check_vma=False,
    )
```

profile of v0, /device:TPU:0, one launch (start us, length us, event | category | flops | bytes accessed | tf_op | source)
XLA Modules:
  0.0 901.3 jit_solution(11002309421669212780)
XLA Ops:
  5.4 48.2 %collective-permute-done = bf16[3,8,360,128]{3,2,1,0:T(8,128)(2,1)} collective-permute-done((bf16[3,8,360,128]{3,2,1,0:T(8,128)(2,1)S(1)}, bf16[3,8,360,128]{3,2,1,0:T(8,128)(2,1)}, u32[]{:S(2)}, u32[]{:S(2)}) %collective-permute-start) | collective-permute-done | bytes 2211872 | tf_op jit(solution)/shard_map/ppermute | solution.py:12
  65.0 52.3 %all-to-all-done = bf16[3,8,360,128]{2,1,0,3:T(8,128)(2,1)S(1)} async-done(((bf16[3,8,360,128]{2,1,0,3:T(8,128)(2,1)}), bf16[3,8,360,128]{2,1,0,3:T(8,128)(2,1)S(1)}, u32[]{:S(2)}, u32[]{:S(2)}) %all-to-all-start) | async-done | bytes 2211872 | tf_op jit(solution)/shard_map/all_to_all | solution.py:82
  128.4 458.1 %while.16 = (s32[]{:T(128)}, f32[3,8,2880,16]{2,3,1,0:T(8,128)}, f32[3,8,2880,16]{2,3,1,0:T(8,128)}, s32[8]{0:T(128)S(1)}, s32[]{:T(128)}, /*index=5*/s32[]{:T(128)}, pred[]{:T(512)}, s32[]{:T(128)}, s32[]{:T(128)}, s32[]{:T(128)}) while((s32[]{:T(128)}, f32[3,8,2880,16]{2,3,1,0:T(8,128)}, f32[3,8,2880,16]{2,3,1,0:T(8,128)}, ...), condition=%wide.region_1.2_spmd.clone, body=%wide.region_0.1_spmd.clone.sunk | while | flops 3414079488 | bytes 76300632 | solution.py:77
  149.8 9.9 %fusion.113 = f32[3,8,128,16]{2,3,1,0:T(8,128)S(1)} fusion(f32[3,8,2880,16]{2,3,1,0:T(8,128)} %get-tuple-element.271, s32[128]{0:T(128)S(1)} %iota_add_fusion.3, f32[8,128]{1,0:T(8,128)S(1)} %multiply_multiply_fusion.2), kind=kOutput, calls=%fused_computation.23.clone.1 | convolution fusion | flops 852713472 | bytes 4624896 | tf_op jit(solution)/shard_map/while/body/eval_jaxpr/frml,mk->frkl/dot_general | solution.py:69
  186.1 9.9 %fusion.113 = f32[3,8,128,16]{2,3,1,0:T(8,128)S(1)} fusion(f32[3,8,2880,16]{2,3,1,0:T(8,128)} %get-tuple-element.271, s32[128]{0:T(128)S(1)} %iota_add_fusion.3, f32[8,128]{1,0:T(8,128)S(1)} %multiply_multiply_fusion.2), kind=kOutput, calls=%fused_computation.23.clone.1 | convolution fusion | flops 852713472 | bytes 4624896 | tf_op jit(solution)/shard_map/while/body/eval_jaxpr/frml,mk->frkl/dot_general | solution.py:69
  211.1 9.2 %bitcast_add_fusion.3 = f32[3,8,2880,16]{2,3,1,0:T(8,128)S(1)} fusion(f32[2880,3,8,16]{0,3,2,1:T(8,128)S(1)} %fusion.112, f32[3,8,2880,16]{2,3,1,0:T(8,128)S(1)} %bitcast.99, f32[3,8,128,16]{2,3,1,0:T(8,128)S(1)} %fusion.113, pred[]{:T(512)S(6)} %compare.3, s32[128]{0:T(128)S(1)} %iota_add_fusion.3), kind=kOutput, calls=%fused_computation.2.clone.1 | convolution fusion | flops 855982080 | bytes 13468161 | tf_op jit(solution)/shard_map/while/body/eval_jaxpr/frkl,mk->frml/dot_general | solution.py:73
  222.5 9.9 %fusion.113 = f32[3,8,128,16]{2,3,1,0:T(8,128)S(1)} fusion(f32[3,8,2880,16]{2,3,1,0:T(8,128)} %get-tuple-element.271, s32[128]{0:T(128)S(1)} %iota_add_fusion.3, f32[8,128]{1,0:T(8,128)S(1)} %multiply_multiply_fusion.2), kind=kOutput, calls=%fused_computation.23.clone.1 | convolution fusion | flops 852713472 | bytes 4624896 | tf_op jit(solution)/shard_map/while/body/eval_jaxpr/frml,mk->frkl/dot_general | solution.py:69
  247.4 9.2 %bitcast_add_fusion.3 = f32[3,8,2880,16]{2,3,1,0:T(8,128)S(1)} fusion(f32[2880,3,8,16]{0,3,2,1:T(8,128)S(1)} %fusion.112, f32[3,8,2880,16]{2,3,1,0:T(8,128)S(1)} %bitcast.99, f32[3,8,128,16]{2,3,1,0:T(8,128)S(1)} %fusion.113, pred[]{:T(512)S(6)} %compare.3, s32[128]{0:T(128)S(1)} %iota_add_fusion.3), kind=kOutput, calls=%fused_computation.2.clone.1 | convolution fusion | flops 855982080 | bytes 13468161 | tf_op jit(solution)/shard_map/while/body/eval_jaxpr/frkl,mk->frml/dot_general | solution.py:73
  258.9 9.9 %fusion.113 = f32[3,8,128,16]{2,3,1,0:T(8,128)S(1)} fusion(f32[3,8,2880,16]{2,3,1,0:T(8,128)} %get-tuple-element.271, s32[128]{0:T(128)S(1)} %iota_add_fusion.3, f32[8,128]{1,0:T(8,128)S(1)} %multiply_multiply_fusion.2), kind=kOutput, calls=%fused_computation.23.clone.1 | convolution fusion | flops 852713472 | bytes 4624896 | tf_op jit(solution)/shard_map/while/body/eval_jaxpr/frml,mk->frkl/dot_general | solution.py:69
  283.8 9.2 %bitcast_add_fusion.3 = f32[3,8,2880,16]{2,3,1,0:T(8,128)S(1)} fusion(f32[2880,3,8,16]{0,3,2,1:T(8,128)S(1)} %fusion.112, f32[3,8,2880,16]{2,3,1,0:T(8,128)S(1)} %bitcast.99, f32[3,8,128,16]{2,3,1,0:T(8,128)S(1)} %fusion.113, pred[]{:T(512)S(6)} %compare.3, s32[128]{0:T(128)S(1)} %iota_add_fusion.3), kind=kOutput, calls=%fused_computation.2.clone.1 | convolution fusion | flops 855982080 | bytes 13468161 | tf_op jit(solution)/shard_map/while/body/eval_jaxpr/frkl,mk->frml/dot_general | solution.py:73
  295.3 9.9 %fusion.113 = f32[3,8,128,16]{2,3,1,0:T(8,128)S(1)} fusion(f32[3,8,2880,16]{2,3,1,0:T(8,128)} %get-tuple-element.271, s32[128]{0:T(128)S(1)} %iota_add_fusion.3, f32[8,128]{1,0:T(8,128)S(1)} %multiply_multiply_fusion.2), kind=kOutput, calls=%fused_computation.23.clone.1 | convolution fusion | flops 852713472 | bytes 4624896 | tf_op jit(solution)/shard_map/while/body/eval_jaxpr/frml,mk->frkl/dot_general | solution.py:69
  320.2 9.2 %bitcast_add_fusion.3 = f32[3,8,2880,16]{2,3,1,0:T(8,128)S(1)} fusion(f32[2880,3,8,16]{0,3,2,1:T(8,128)S(1)} %fusion.112, f32[3,8,2880,16]{2,3,1,0:T(8,128)S(1)} %bitcast.99, f32[3,8,128,16]{2,3,1,0:T(8,128)S(1)} %fusion.113, pred[]{:T(512)S(6)} %compare.3, s32[128]{0:T(128)S(1)} %iota_add_fusion.3), kind=kOutput, calls=%fused_computation.2.clone.1 | convolution fusion | flops 855982080 | bytes 13468161 | tf_op jit(solution)/shard_map/while/body/eval_jaxpr/frkl,mk->frml/dot_general | solution.py:73
  331.6 9.9 %fusion.113 = f32[3,8,128,16]{2,3,1,0:T(8,128)S(1)} fusion(f32[3,8,2880,16]{2,3,1,0:T(8,128)} %get-tuple-element.271, s32[128]{0:T(128)S(1)} %iota_add_fusion.3, f32[8,128]{1,0:T(8,128)S(1)} %multiply_multiply_fusion.2), kind=kOutput, calls=%fused_computation.23.clone.1 | convolution fusion | flops 852713472 | bytes 4624896 | tf_op jit(solution)/shard_map/while/body/eval_jaxpr/frml,mk->frkl/dot_general | solution.py:69
  356.5 9.2 %bitcast_add_fusion.3 = f32[3,8,2880,16]{2,3,1,0:T(8,128)S(1)} fusion(f32[2880,3,8,16]{0,3,2,1:T(8,128)S(1)} %fusion.112, f32[3,8,2880,16]{2,3,1,0:T(8,128)S(1)} %bitcast.99, f32[3,8,128,16]{2,3,1,0:T(8,128)S(1)} %fusion.113, pred[]{:T(512)S(6)} %compare.3, s32[128]{0:T(128)S(1)} %iota_add_fusion.3), kind=kOutput, calls=%fused_computation.2.clone.1 | convolution fusion | flops 855982080 | bytes 13468161 | tf_op jit(solution)/shard_map/while/body/eval_jaxpr/frkl,mk->frml/dot_general | solution.py:73
  368.0 9.9 %fusion.113 = f32[3,8,128,16]{2,3,1,0:T(8,128)S(1)} fusion(f32[3,8,2880,16]{2,3,1,0:T(8,128)} %get-tuple-element.271, s32[128]{0:T(128)S(1)} %iota_add_fusion.3, f32[8,128]{1,0:T(8,128)S(1)} %multiply_multiply_fusion.2), kind=kOutput, calls=%fused_computation.23.clone.1 | convolution fusion | flops 852713472 | bytes 4624896 | tf_op jit(solution)/shard_map/while/body/eval_jaxpr/frml,mk->frkl/dot_general | solution.py:69
  404.4 9.9 %fusion.113 = f32[3,8,128,16]{2,3,1,0:T(8,128)S(1)} fusion(f32[3,8,2880,16]{2,3,1,0:T(8,128)} %get-tuple-element.271, s32[128]{0:T(128)S(1)} %iota_add_fusion.3, f32[8,128]{1,0:T(8,128)S(1)} %multiply_multiply_fusion.2), kind=kOutput, calls=%fused_computation.23.clone.1 | convolution fusion | flops 852713472 | bytes 4624896 | tf_op jit(solution)/shard_map/while/body/eval_jaxpr/frml,mk->frkl/dot_general | solution.py:69
  440.7 9.9 %fusion.113 = f32[3,8,128,16]{2,3,1,0:T(8,128)S(1)} fusion(f32[3,8,2880,16]{2,3,1,0:T(8,128)} %get-tuple-element.271, s32[128]{0:T(128)S(1)} %iota_add_fusion.3, f32[8,128]{1,0:T(8,128)S(1)} %multiply_multiply_fusion.2), kind=kOutput, calls=%fused_computation.23.clone.1 | convolution fusion | flops 852713472 | bytes 4624896 | tf_op jit(solution)/shard_map/while/body/eval_jaxpr/frml,mk->frkl/dot_general | solution.py:69
  477.1 9.9 %fusion.113 = f32[3,8,128,16]{2,3,1,0:T(8,128)S(1)} fusion(f32[3,8,2880,16]{2,3,1,0:T(8,128)} %get-tuple-element.271, s32[128]{0:T(128)S(1)} %iota_add_fusion.3, f32[8,128]{1,0:T(8,128)S(1)} %multiply_multiply_fusion.2), kind=kOutput, calls=%fused_computation.23.clone.1 | convolution fusion | flops 852713472 | bytes 4624896 | tf_op jit(solution)/shard_map/while/body/eval_jaxpr/frml,mk->frkl/dot_general | solution.py:69
  513.5 9.9 %fusion.113 = f32[3,8,128,16]{2,3,1,0:T(8,128)S(1)} fusion(f32[3,8,2880,16]{2,3,1,0:T(8,128)} %get-tuple-element.271, s32[128]{0:T(128)S(1)} %iota_add_fusion.3, f32[8,128]{1,0:T(8,128)S(1)} %multiply_multiply_fusion.2), kind=kOutput, calls=%fused_computation.23.clone.1 | convolution fusion | flops 852713472 | bytes 4624896 | tf_op jit(solution)/shard_map/while/body/eval_jaxpr/frml,mk->frkl/dot_general | solution.py:69
  549.8 9.9 %fusion.113 = f32[3,8,128,16]{2,3,1,0:T(8,128)S(1)} fusion(f32[3,8,2880,16]{2,3,1,0:T(8,128)} %get-tuple-element.271, s32[128]{0:T(128)S(1)} %iota_add_fusion.3, f32[8,128]{1,0:T(8,128)S(1)} %multiply_multiply_fusion.2), kind=kOutput, calls=%fused_computation.23.clone.1 | convolution fusion | flops 852713472 | bytes 4624896 | tf_op jit(solution)/shard_map/while/body/eval_jaxpr/frml,mk->frkl/dot_general | solution.py:69
  574.8 9.2 %bitcast_add_fusion.3 = f32[3,8,2880,16]{2,3,1,0:T(8,128)S(1)} fusion(f32[2880,3,8,16]{0,3,2,1:T(8,128)S(1)} %fusion.112, f32[3,8,2880,16]{2,3,1,0:T(8,128)S(1)} %bitcast.99, f32[3,8,128,16]{2,3,1,0:T(8,128)S(1)} %fusion.113, pred[]{:T(512)S(6)} %compare.3, s32[128]{0:T(128)S(1)} %iota_add_fusion.3), kind=kOutput, calls=%fused_computation.2.clone.1 | convolution fusion | flops 855982080 | bytes 13468161 | tf_op jit(solution)/shard_map/while/body/eval_jaxpr/frkl,mk->frml/dot_general | solution.py:73
  590.6 15.0 %copy.38 = bf16[3,8,2880,16]{3,1,0,2:T(8,128)(2,1)} copy(bf16[3,8,2880,16]{2,3,1,0:T(8,128)(2,1)S(1)} %add_convert_fusion) | data formatting | bytes 4423680 | tf_op jit(solution)/shard_map/convert_element_type | solution.py:87
  605.6 19.4 %reshape.151 = bf16[8,2,69120]{2,1,0:T(2,128)(2,1)S(1)} reshape(bf16[2880,3,8,16]{3,2,1,0:T(8,128)(2,1)} %bitcast.102) | data formatting | bytes 4423680
  625.0 55.0 %all_to_all.27 = bf16[8,2,69120]{2,1,0:T(2,128)(2,1)} all-to-all(bf16[8,2,69120]{2,1,0:T(2,128)(2,1)S(1)} %reshape.151), channel_id=1, replica_groups=mesh['lat'=4,'lon'=8] {'lon'}, dimensions={0} | all-to-all | bytes 4423680 | tf_op jit(solution)/shard_map/all_to_all | solution.py:88
  680.0 14.6 %reshape.152 = bf16[2880,3,8,16]{3,2,1,0:T(8,128)(2,1)} reshape(bf16[8,2,69120]{2,1,0:T(2,128)(2,1)} %all_to_all.27) | data formatting | bytes 4423680
  694.6 17.9 %copy.39 = bf16[3,8,8,360,16]{3,4,2,1,0:T(8,128)(2,1)S(1)} copy(bf16[3,8,8,360,16]{4,1,0,3,2:T(8,128)(2,1)} %bitcast.103) | data formatting | bytes 4423680 | tf_op jit(solution)/shard_map/all_to_all | solution.py:88
  730.5 15.3 %copy.51 = f32[5,16,360,128]{2,3,1,0:T(8,128)} copy(f32[5,16,360,128]{3,2,1,0:T(8,128)} %param.9) | data formatting | bytes 29491200 | tf_op args[3]
  745.8 10.1 %convert.13 = bf16[5,16,360,128]{2,3,1,0:T(8,128)(2,1)} convert(f32[5,16,360,128]{2,3,1,0:T(8,128)} %copy.51) | non-fusion elementwise | flops 3686400 | bytes 22118400 | tf_op jit(solution)/shard_map/convert.5
  813.8 14.1 %maximum_convert_fusion.1 = f32[6,16,362,128]{2,3,1,0:T(8,128)} fusion(bf16[6,16,1,128]{2,3,1,0:T(8,128)(2,1)} %copy.48, bf16[1,16,360,128]{2,3,1,0:T(8,128)(2,1)} %copy-done.6, bf16[5,16,360,128]{2,3,1,0:T(8,128)(2,1)} %convert.13, bf16[6,16,1,128]{2,3,1,0:T(8,128)(2,1)S(1)} %copy.47), kind=kLoop, calls=%fused_computation.74 | loop fusion | flops 35586048 | bytes 26689536 | tf_op jit(solution)/shard_map/convert_element_type | solution.py:123
  838.0 15.0 %maximum_convert_fusion = f32[6,18,360,128]{2,3,1,0:T(8,128)} fusion(bf16[6,1,360,128]{2,3,1,0:T(8,128)(2,1)S(1)} %copy-done.9, bf16[1,16,360,128]{2,3,1,0:T(8,128)(2,1)S(1)} %copy-done.5, bf16[5,16,360,128]{2,3,1,0:T(8,128)(2,1)} %convert.13, bf16[6,1,360,128]{2,3,1,0:T(8,128)(2,1)S(1)} %copy-done.10), kind=kLoop, calls=%fused_computation.72 | loop fusion | flops 19906560 | bytes 29859840 | tf_op jit(solution)/shard_map/convert_element_type | solution.py:119
  853.7 32.1 %fusion.68 = f32[5,16,360,128]{2,3,1,0:T(8,128)} fusion(f32[6,18,360,128]{2,3,1,0:T(8,128)} %maximum_convert_fusion, f32[5,16,360,128]{2,3,1,0:T(8,128)S(1)} %bitcast.101, f32[6,16,362,128]{2,3,1,0:T(8,128)} %maximum_convert_fusion.1, f32[16]{0:T(128)S(1)} %get-tuple-element.202, f32[16,360,128]{1,2,0:T(8,128)} %get-tuple-element.198, ...), kind=kLoop, calls=%fused_computation.62 | loop fusion | flops 70041600 | bytes 112066752 | tf_op jit(solution)/shard_map/sub | solution.py:140
  885.8 15.3 %copy.59 = f32[5,16,360,128]{3,2,1,0:T(8,128)} copy(f32[5,16,360,128]{2,3,1,0:T(8,128)} %fusion.68) | data formatting | bytes 29491200
  (270 shorter events, 379.5 us)
Async XLA Ops:
  0.6 63.7 %copy-start = (s32[64]{0:T(128)S(1)}, s32[64]{0:T(128)}, u32[]{:S(2)}) copy-start(s32[64]{0:T(128)} %param.7) | copy-start | bytes 772
  2.4 51.2 %collective-permute-start = (bf16[3,8,360,128]{3,2,1,0:T(8,128)(2,1)S(1)}, bf16[3,8,360,128]{3,2,1,0:T(8,128)(2,1)}, u32[]{:S(2)}, u32[]{:S(2)}) collective-permute-start(bf16[3,8,360,128]{3,2,1,0:T(8,128)(2,1)S(1)} %slice.46), channel_id=1, source_target_pairs={{0,16},{8,24},{16,0},{24,8},{1,17},{9,25},{17,1},{25,9},{2,18},{10... | collective-permute-start | bytes 6635528 | tf_op jit(solution)/shard_map/ppermute | solution.py:12
  58.2 59.1 %all-to-all-start = ((bf16[3,8,360,128]{2,1,0,3:T(8,128)(2,1)}), bf16[3,8,360,128]{2,1,0,3:T(8,128)(2,1)S(1)}, u32[]{:S(2)}, u32[]{:S(2)}) async-start(bf16[3,8,360,128]{2,1,0,3:T(8,128)(2,1)} %copy.35), calls=%async_computation | async-start | bytes 4718592 | tf_op jit(solution)/shard_map/all_to_all | solution.py:82
  149.8 24.9 %slice-start.2 = ((s8[4521984]{0:T(1024)(128)(4,1)}), s8[4194304]{0:T(1024)(128)(4,1)S(1)}, s32[]{:S(2)}) async-start(s8[4521984]{0:T(1024)(128)(4,1)} %bitcast.98), calls=%async_computation.4 | async-start | bytes 8388608 | tf_op jit(solution)/shard_map/while
  186.1 24.9 %slice-start.2 = ((s8[4521984]{0:T(1024)(128)(4,1)}), s8[4194304]{0:T(1024)(128)(4,1)S(1)}, s32[]{:S(2)}) async-start(s8[4521984]{0:T(1024)(128)(4,1)} %bitcast.98), calls=%async_computation.4 | async-start | bytes 8388608 | tf_op jit(solution)/shard_map/while
  196.0 15.0 %slice-start.3 = ((s8[4521984]{0:T(1024)(128)(4,1)}), s8[327680]{0:T(1024)(128)(4,1)S(1)}, s32[]{:S(2)}) async-start(s8[4521984]{0:T(1024)(128)(4,1)} %bitcast.98), calls=%async_computation.5 | async-start | bytes 655360 | tf_op jit(solution)/shard_map/while
  222.5 24.9 %slice-start.2 = ((s8[4521984]{0:T(1024)(128)(4,1)}), s8[4194304]{0:T(1024)(128)(4,1)S(1)}, s32[]{:S(2)}) async-start(s8[4521984]{0:T(1024)(128)(4,1)} %bitcast.98), calls=%async_computation.4 | async-start | bytes 8388608 | tf_op jit(solution)/shard_map/while
  232.4 15.0 %slice-start.3 = ((s8[4521984]{0:T(1024)(128)(4,1)}), s8[327680]{0:T(1024)(128)(4,1)S(1)}, s32[]{:S(2)}) async-start(s8[4521984]{0:T(1024)(128)(4,1)} %bitcast.98), calls=%async_computation.5 | async-start | bytes 655360 | tf_op jit(solution)/shard_map/while
  258.9 24.9 %slice-start.2 = ((s8[4521984]{0:T(1024)(128)(4,1)}), s8[4194304]{0:T(1024)(128)(4,1)S(1)}, s32[]{:S(2)}) async-start(s8[4521984]{0:T(1024)(128)(4,1)} %bitcast.98), calls=%async_computation.4 | async-start | bytes 8388608 | tf_op jit(solution)/shard_map/while
  268.8 15.0 %slice-start.3 = ((s8[4521984]{0:T(1024)(128)(4,1)}), s8[327680]{0:T(1024)(128)(4,1)S(1)}, s32[]{:S(2)}) async-start(s8[4521984]{0:T(1024)(128)(4,1)} %bitcast.98), calls=%async_computation.5 | async-start | bytes 655360 | tf_op jit(solution)/shard_map/while
  295.2 24.9 %slice-start.2 = ((s8[4521984]{0:T(1024)(128)(4,1)}), s8[4194304]{0:T(1024)(128)(4,1)S(1)}, s32[]{:S(2)}) async-start(s8[4521984]{0:T(1024)(128)(4,1)} %bitcast.98), calls=%async_computation.4 | async-start | bytes 8388608 | tf_op jit(solution)/shard_map/while
  305.2 15.0 %slice-start.3 = ((s8[4521984]{0:T(1024)(128)(4,1)}), s8[327680]{0:T(1024)(128)(4,1)S(1)}, s32[]{:S(2)}) async-start(s8[4521984]{0:T(1024)(128)(4,1)} %bitcast.98), calls=%async_computation.5 | async-start | bytes 655360 | tf_op jit(solution)/shard_map/while
  331.6 24.9 %slice-start.2 = ((s8[4521984]{0:T(1024)(128)(4,1)}), s8[4194304]{0:T(1024)(128)(4,1)S(1)}, s32[]{:S(2)}) async-start(s8[4521984]{0:T(1024)(128)(4,1)} %bitcast.98), calls=%async_computation.4 | async-start | bytes 8388608 | tf_op jit(solution)/shard_map/while
  341.5 15.0 %slice-start.3 = ((s8[4521984]{0:T(1024)(128)(4,1)}), s8[327680]{0:T(1024)(128)(4,1)S(1)}, s32[]{:S(2)}) async-start(s8[4521984]{0:T(1024)(128)(4,1)} %bitcast.98), calls=%async_computation.5 | async-start | bytes 655360 | tf_op jit(solution)/shard_map/while
  368.0 24.9 %slice-start.2 = ((s8[4521984]{0:T(1024)(128)(4,1)}), s8[4194304]{0:T(1024)(128)(4,1)S(1)}, s32[]{:S(2)}) async-start(s8[4521984]{0:T(1024)(128)(4,1)} %bitcast.98), calls=%async_computation.4 | async-start | bytes 8388608 | tf_op jit(solution)/shard_map/while
  404.4 24.9 %slice-start.2 = ((s8[4521984]{0:T(1024)(128)(4,1)}), s8[4194304]{0:T(1024)(128)(4,1)S(1)}, s32[]{:S(2)}) async-start(s8[4521984]{0:T(1024)(128)(4,1)} %bitcast.98), calls=%async_computation.4 | async-start | bytes 8388608 | tf_op jit(solution)/shard_map/while
  440.7 24.9 %slice-start.2 = ((s8[4521984]{0:T(1024)(128)(4,1)}), s8[4194304]{0:T(1024)(128)(4,1)S(1)}, s32[]{:S(2)}) async-start(s8[4521984]{0:T(1024)(128)(4,1)} %bitcast.98), calls=%async_computation.4 | async-start | bytes 8388608 | tf_op jit(solution)/shard_map/while
  450.6 15.0 %slice-start.3 = ((s8[4521984]{0:T(1024)(128)(4,1)}), s8[327680]{0:T(1024)(128)(4,1)S(1)}, s32[]{:S(2)}) async-start(s8[4521984]{0:T(1024)(128)(4,1)} %bitcast.98), calls=%async_computation.5 | async-start | bytes 655360 | tf_op jit(solution)/shard_map/while
  477.1 24.9 %slice-start.2 = ((s8[4521984]{0:T(1024)(128)(4,1)}), s8[4194304]{0:T(1024)(128)(4,1)S(1)}, s32[]{:S(2)}) async-start(s8[4521984]{0:T(1024)(128)(4,1)} %bitcast.98), calls=%async_computation.4 | async-start | bytes 8388608 | tf_op jit(solution)/shard_map/while
  513.5 24.9 %slice-start.2 = ((s8[4521984]{0:T(1024)(128)(4,1)}), s8[4194304]{0:T(1024)(128)(4,1)S(1)}, s32[]{:S(2)}) async-start(s8[4521984]{0:T(1024)(128)(4,1)} %bitcast.98), calls=%async_computation.4 | async-start | bytes 8388608 | tf_op jit(solution)/shard_map/while
  549.8 24.9 %slice-start.2 = ((s8[4521984]{0:T(1024)(128)(4,1)}), s8[4194304]{0:T(1024)(128)(4,1)S(1)}, s32[]{:S(2)}) async-start(s8[4521984]{0:T(1024)(128)(4,1)} %bitcast.98), calls=%async_computation.4 | async-start | bytes 8388608 | tf_op jit(solution)/shard_map/while
  559.8 15.0 %slice-start.3 = ((s8[4521984]{0:T(1024)(128)(4,1)}), s8[327680]{0:T(1024)(128)(4,1)S(1)}, s32[]{:S(2)}) async-start(s8[4521984]{0:T(1024)(128)(4,1)} %bitcast.98), calls=%async_computation.5 | async-start | bytes 655360 | tf_op jit(solution)/shard_map/while
  715.2 49.0 %collective-permute-start.1 = (bf16[3,8,360,128]{3,2,1,0:T(8,128)(2,1)}, bf16[3,8,360,128]{3,2,1,0:T(8,128)(2,1)}, u32[]{:S(2)}, u32[]{:S(2)}) collective-permute-start(bf16[3,8,360,128]{3,2,1,0:T(8,128)(2,1)} %copy.40), channel_id=1, source_target_pairs={{0,16},{8,24},{16,0},{24,8},{1,17},{9,25},{17,1},{25,9},{2,18},{10... | collective-permute-start | bytes 6635528 | tf_op jit(solution)/shard_map/ppermute | solution.py:12
  790.7 20.3 %collective-permute-start.3 = (bf16[6,16,1,128]{3,1,2,0:T(8,128)(2,1)S(1)}, bf16[6,16,1,128]{3,1,2,0:T(8,128)(2,1)S(1)}, u32[]{:S(2)}, u32[]{:S(2)}) collective-permute-start(bf16[6,16,1,128]{3,1,2,0:T(8,128)(2,1)S(1)} %copy.46), channel_id=1, source_target_pairs={{1,0},{2,1},{3,2},{4,3},{5,4},{6,5},{7,6},{0,7},{9,8},{10,9},{11,1... | collective-permute-start | bytes 73736 | tf_op jit(solution)/shard_map/ppermute | solution.py:25
  794.0 15.2 %collective-permute-start.2 = (bf16[6,16,1,128]{3,1,2,0:T(8,128)(2,1)S(1)}, bf16[6,16,1,128]{3,1,2,0:T(8,128)(2,1)S(1)}, u32[]{:S(2)}, u32[]{:S(2)}) collective-permute-start(bf16[6,16,1,128]{3,1,2,0:T(8,128)(2,1)S(1)} %copy.45), channel_id=1, source_target_pairs={{0,1},{1,2},{2,3},{3,4},{4,5},{5,6},{6,7},{7,0},{8,9},{9,10},{10,1... | collective-permute-start | bytes 73736 | tf_op jit(solution)/shard_map/ppermute | solution.py:22
  804.0 23.9 %collective-permute-start.5 = (bf16[6,1,360,128]{3,2,1,0:T(8,128)(2,1)}, bf16[6,1,360,128]{3,2,1,0:T(8,128)(2,1)}, u32[]{:S(2)}, u32[]{:S(2)}) collective-permute-start(bf16[6,1,360,128]{3,2,1,0:T(8,128)(2,1)} %copy.53), channel_id=1, source_target_pairs={{8,0},{16,8},{24,16},{9,1},{17,9},{25,17},{10,2},{18,10},{26,18},{... | collective-permute-start | bytes 1658888 | tf_op jit(solution)/shard_map/ppermute | solution.py:25
  805.3 24.7 %collective-permute-start.4 = (bf16[6,1,360,128]{3,2,1,0:T(8,128)(2,1)}, bf16[6,1,360,128]{3,2,1,0:T(8,128)(2,1)}, u32[]{:S(2)}, u32[]{:S(2)}) collective-permute-start(bf16[6,1,360,128]{3,2,1,0:T(8,128)(2,1)} %copy.52), channel_id=1, source_target_pairs={{0,8},{8,16},{16,24},{1,9},{9,17},{17,25},{2,10},{10,18},{18,26},{... | collective-permute-start | bytes 1658888 | tf_op jit(solution)/shard_map/ppermute | solution.py:22
  832.2 21.5 %slice-start.4 = ((s8[15728640]{0:T(1024)(128)(4,1)}), s8[4194304]{0:T(1024)(128)(4,1)S(1)}, s32[]{:S(2)}) async-start(s8[15728640]{0:T(1024)(128)(4,1)} %bitcast.100), calls=%async_computation.6 | async-start | bytes 8388608
  832.2 21.5 %slice-start.5 = ((s8[15728640]{0:T(1024)(128)(4,1)}), s8[4194304]{0:T(1024)(128)(4,1)S(1)}, s32[]{:S(2)}) async-start(s8[15728640]{0:T(1024)(128)(4,1)} %bitcast.100), calls=%async_computation.7 | async-start | bytes 8388608
  838.0 15.7 %slice-start.6 = ((s8[15728640]{0:T(1024)(128)(4,1)}), s8[4194304]{0:T(1024)(128)(4,1)S(1)}, s32[]{:S(2)}) async-start(s8[15728640]{0:T(1024)(128)(4,1)} %bitcast.100), calls=%async_computation.8 | async-start | bytes 8388608
  838.0 15.7 %slice-start.7 = ((s8[15728640]{0:T(1024)(128)(4,1)}), s8[3145728]{0:T(1024)(128)(4,1)S(1)}, s32[]{:S(2)}) async-start(s8[15728640]{0:T(1024)(128)(4,1)} %bitcast.100), calls=%async_computation.9 | async-start | bytes 6291456
  885.8 15.3 %copy-start.1 = (s32[64]{0:T(128)S(1)}, s32[64]{0:T(128)}, u32[]{:S(2)}) copy-start(s32[64]{0:T(128)} %param.7) | copy-start | bytes 772
  (40 other events, 293.5 us)
where the time goes:
time: 908 us; the launch traced here: 901 us
  matrix products  409 us (45%)
  local copies, waits for them, and re-layouts  184 us (20%)
  waiting for transfers between devices  109 us (12%)
  other arithmetic  101 us (11%)
  blocking collectives  55 us (6%)
  loops' own time  22.6 us (2%)
  starting transfers between devices  19.7 us (2%)
    dot_general x12, matrix products, one_block(): jnp.einsum('frml,mk->frkl', row_data, sin_table, precision=lax.Precision....  119 us
    dot_general x12, matrix products, one_block(): jnp.einsum('frkl,mk->frml', sin_part * weights, sin_table, precision=lax....  111 us
    dot_general x12, matrix products, one_block(): jnp.einsum('frml,mk->frkl', row_data, cos_table, precision=lax.Precision....  90 us
    dot_general x12, matrix products, one_block(): jnp.einsum('frkl,mk->frml', cos_part * weights, cos_table, precision=lax....  89.5 us
    unnamed x41, local copies, waits for them, and re-layouts  85.5 us
    ppermute x2, waiting for transfers between devices, swapped(): lax.ppermute(array, axis, [(i, i ^ 1 << apart) for i in range(lax.axis_si...  56.5 us
    all_to_all x1, blocking collectives, polar_filter(): lax.all_to_all(filtered_rows, 'lon', split_axis=2, concat_axis=3, tiled=T...  55 us
    all_to_all x1, waiting for transfers between devices, polar_filter(): lax.all_to_all(work_rows, 'lon', split_axis=3, concat_axis=2, tiled=True)  52.3 us
  transfers between devices with their start and end apart: 7, of which 3 were waited for; matrix products, arithmetic and copies ran while one was open for 8% of the time, Pallas kernels for 0%

commit v1 on v0

v1 whole, which is shorter than its diff:
```python
import functools
import math

import jax
import jax.numpy as jnp
import numpy as np
from jax import lax
from jax.experimental import pallas as pl
from jax.experimental.pallas import tpu as pltpu
from jax.sharding import PartitionSpec as P

HEMI = 720
CHUNK = 24
VMEM_BYTES = 48 * 1024 * 1024
FACTOR_FLOOR = 1e-7


def latitude_factors(row_ids, lat_count):
    grid_row = row_ids.astype(jnp.float32) + jnp.float32(HEMI // 2 - lat_count // 2)
    centre_cos = jnp.sin(math.pi * (grid_row + 0.5) / (2.0 * HEMI))
    face_cos = jnp.sin(math.pi * grid_row / (2.0 * HEMI))
    return (centre_cos, face_cos)


@functools.lru_cache(maxsize=None)
def cosecant_factors(lon_count, width):
    cells = np.arange(width)
    apart = cells[:, None] - cells[None, :]
    safe = np.where(apart == 0, 1, apart)
    own = np.where(apart == 0, 0.0, 1.0 / (lon_count * np.sin(np.pi * safe / lon_count)))
    targets, sources, shifts = [], [], []
    for shift in range(1, lon_count // width):
        block = 1.0 / (lon_count * np.sin(np.pi * (apart + shift * width) / lon_count))
        left, values, right = np.linalg.svd(block)
        rank = max(4, -4 * (-int((values > FACTOR_FLOOR).sum()) // 4))
        root = np.sqrt(values[:rank])
        targets.append(np.tile(left[:, :rank] * root, (1, 2)))
        sources.append(np.tile(root[:, None] * right[:rank], (2, 1)))
        shifts.append((shift, rank))
    return own, np.concatenate(targets, 1), np.concatenate(sources, 0), tuple(shifts)


def filter_tables(odd, strength, lon_count, width):
    own, targets, sources, shifts = cosecant_factors(lon_count, width)

    def phase(cells):
        return (odd[:, None] * cells[None, :] % (2 * lon_count)).astype(jnp.float32) * (
            math.pi / lon_count
        )

    here = phase(jnp.arange(width, dtype=jnp.int32))
    sin_here, cos_here = jnp.sin(here), jnp.cos(here)
    near = (
        sin_here[:, :, None] * cos_here[:, None, :] - cos_here[:, :, None] * sin_here[:, None, :]
    ) * jnp.asarray(own, jnp.float32)
    near = near + jnp.eye(width, dtype=jnp.float32) * (odd.astype(jnp.float32) / lon_count)[
        :, None, None
    ]
    near = (near * strength[:, None, None]).astype(jnp.bfloat16)
    offsets = np.concatenate([np.full(2 * rank, shift * width) for shift, rank in shifts])
    is_sin = np.concatenate([np.repeat([False, True], rank) for _, rank in shifts])
    moved = phase(jnp.asarray(offsets, jnp.int32)) - jnp.asarray(
        np.where(is_sin, math.pi / 2, 0.0), jnp.float32
    )
    far = sin_here[:, :, None] * jnp.cos(moved)[:, None, :] + cos_here[:, :, None] * jnp.sin(moved)[
        :, None, :
    ]
    far = (far * jnp.asarray(targets, jnp.float32) * strength[:, None, None]).astype(jnp.bfloat16)
    send = jnp.where(is_sin[None, :, None], sin_here[:, None, :], cos_here[:, None, :])
    send = (send * jnp.asarray(sources, jnp.float32)).astype(jnp.bfloat16)
    return near, far, send, shifts


def project_kernel(x_ref, send_ref, out_ref):
    row = jnp.concatenate([x_ref[f, 0] for f in range(x_ref.shape[0])], axis=1)
    out_ref[0] = jnp.dot(send_ref[0], row, preferred_element_type=jnp.float32).astype(out_ref.dtype)


def project(tendencies, send):
    fields, rows, width, lev = tendencies.shape
    count = send.shape[1]
    return pl.pallas_call(
        project_kernel,
        grid=(rows,),
        in_specs=[
            pl.BlockSpec((fields, 1, width, lev), lambda j: (0, j, 0, 0)),
            pl.BlockSpec((1, count, width), lambda j: (j, 0, 0)),
        ],
        out_specs=pl.BlockSpec((1, count, fields * lev), lambda j: (j, 0, 0)),
        out_shape=jax.ShapeDtypeStruct((rows, count, fields * lev), jnp.bfloat16),
        compiler_params=pltpu.CompilerParams(vmem_limit_bytes=VMEM_BYTES),
        cost_estimate=pl.CostEstimate(
            flops=2 * rows * count * width * fields * lev,
            bytes_accessed=2 * tendencies.size + 2 * send.size,
            transcendentals=0,
        ),
        name="project_tendencies",
    )(tendencies, send)


def filter_kernel(keep_ref, x_ref, near_ref, far_ref, coef_ref, winds_ref, filtered_ref, courant_ref):
    fields, _, _, lev = x_ref.shape
    keep = keep_ref[pl.program_id(0)]
    row = jnp.concatenate([x_ref[f, 0] for f in range(fields)], axis=1)
    total = jnp.dot(near_ref[0], row, preferred_element_type=jnp.float32)
    total = total + jnp.dot(far_ref[0], coef_ref[0], preferred_element_type=jnp.float32)
    for f in range(fields):
        value = keep * x_ref[f, 0].astype(jnp.float32) + total[:, f * lev : (f + 1) * lev]
        value = value.astype(jnp.bfloat16)
        filtered_ref[f, 0] = value
        if f < 2:
            wind = winds_ref[f, 0] + value.astype(jnp.float32)
            courant_ref[f, 0] = (0.5 if f == 0 else 0.25) * jnp.tanh(wind)


def filter_rows(keep, tendencies, near, far, coefs, winds):
    fields, rows, width, lev = tendencies.shape
    count = far.shape[2]
    return pl.pallas_call(
        filter_kernel,
        grid=(rows,),
        in_specs=[
            pl.BlockSpec(memory_space=pltpu.SMEM),
            pl.BlockSpec((fields, 1, width, lev), lambda j: (0, j, 0, 0)),
            pl.BlockSpec((1, width, width), lambda j: (j, 0, 0)),
            pl.BlockSpec((1, width, count), lambda j: (j, 0, 0)),
            pl.BlockSpec((1, count, fields * lev), lambda j: (j, 0, 0)),
            pl.BlockSpec((2, 1, width, lev), lambda j: (0, j, 0, 0)),
        ],
        out_specs=[
            pl.BlockSpec((fields, 1, width, lev), lambda j: (0, j, 0, 0)),
            pl.BlockSpec((2, 1, width, lev), lambda j: (0, j, 0, 0)),
        ],
        out_shape=[
            jax.ShapeDtypeStruct(tendencies.shape, jnp.bfloat16),
            jax.ShapeDtypeStruct(winds.shape, jnp.float32),
        ],
        compiler_params=pltpu.CompilerParams(vmem_limit_bytes=VMEM_BYTES),
        cost_estimate=pl.CostEstimate(
            flops=2 * rows * (width + count) * width * fields * lev,
            bytes_accessed=4 * tendencies.size + 8 * winds.size,
            transcendentals=winds.size,
        ),
        name="filter_rows",
    )(keep, tendencies, near, far, coefs, winds)


def advect_kernel(
    face_ref, inverse_ref, tracer_ref, courant_ref, prior_ref, next_ref, west_ref, east_ref,
    north_ref, zonal_ref, out_ref, before, partial, edge, shifted,
):
    tracers, _, width, _ = tracer_ref.shape
    step = pl.program_id(0)
    rows = pl.num_programs(0) - 1
    face = face_ref[step]
    inverse_before = inverse_ref[jnp.maximum(step - 1, 0)]
    chunks = [(start, min(CHUNK, width - start)) for start in range(0, width, CHUNK)]

    @pl.when(step == 0)
    def _():
        before[...] = prior_ref[:, 0]
        partial[...] = jnp.zeros_like(partial)

    @pl.when(step < rows)
    def _():
        inverse = inverse_ref[jnp.minimum(step, rows - 1)]
        shifted[0:width, :] = courant_ref[0, 0]
        shifted[width : width + 1, :] = zonal_ref[0]
        for start, size in chunks:
            part = pl.ds(start, size)
            here = courant_ref[0, 0, part, :]
            there = shifted[pl.ds(start + 1, size), :]
            north = courant_ref[1, 0, part, :]
            here_up, here_down = jnp.maximum(here, 0.0), jnp.minimum(here, 0.0)
            there_up, there_down = jnp.maximum(there, 0.0), jnp.minimum(there, 0.0)
            north_up = face * jnp.maximum(north, 0.0)
            north_down = face * jnp.minimum(north, 0.0)
            for q in range(tracers):
                value = tracer_ref[q, 0, part, :]
                if start == 0:
                    edge[q, 7:8, :] = west_ref[q, 0]
                    edge[q, pl.ds(8, size), :] = value
                    west = edge[q, pl.ds(7, size), :]
                else:
                    west = tracer_ref[q, 0, pl.ds(start - 1, size), :]
                if start + size == width:
                    edge[q, pl.ds(8, size), :] = value
                    edge[q, pl.ds(8 + size, 1), :] = east_ref[q, 0]
                    east = edge[q, pl.ds(9, size), :]
                else:
                    east = tracer_ref[q, 0, pl.ds(start + 1, size), :]
                flux = north_up * before[q, part, :] + north_down * value
                out_ref[q, 0, part, :] = partial[q, part, :] - flux * inverse_before
                zonal = (there_up * value + there_down * east) - (here_up * west + here_down * value)
                partial[q, part, :] = value - zonal + flux * inverse
                before[q, part, :] = value

    @pl.when(step == rows)
    def _():
        for start, size in chunks:
            part = pl.ds(start, size)
            north = north_ref[part, :]
            north_up = face * jnp.maximum(north, 0.0)
            north_down = face * jnp.minimum(north, 0.0)
            for q in range(tracers):
                flux = north_up * before[q, part, :] + north_down * next_ref[q, 0, part, :]
                out_ref[q, 0, part, :] = partial[q, part, :] - flux * inverse_before


def advect(face, inverse, tracers, courants, prior, following, west, east, north, zonal):
    count, rows, width, lev = tracers.shape

    def clipped(j):
        return jnp.minimum(j, rows - 1)

    row_halo = pl.BlockSpec((count, 1, width, lev), lambda j: (0, 0, 0, 0))
    column_halo = pl.BlockSpec((count, 1, 1, lev), lambda j: (0, clipped(j), 0, 0))
    return pl.pallas_call(
        advect_kernel,
        grid=(rows + 1,),
        in_specs=[
            pl.BlockSpec(memory_space=pltpu.SMEM),
            pl.BlockSpec(memory_space=pltpu.SMEM),
            pl.BlockSpec((count, 1, width, lev), lambda j: (0, clipped(j), 0, 0)),
            pl.BlockSpec((2, 1, width, lev), lambda j: (0, clipped(j), 0, 0)),
            row_halo,
            row_halo,
            column_halo,
            column_halo,
            pl.BlockSpec((width, lev), lambda j: (0, 0)),
            pl.BlockSpec((1, 1, lev), lambda j: (clipped(j), 0, 0)),
        ],
        out_specs=pl.BlockSpec((count, 1, width, lev), lambda j: (0, jnp.maximum(j - 1, 0), 0, 0)),
        out_shape=jax.ShapeDtypeStruct(tracers.shape, jnp.float32),
        scratch_shapes=[
            pltpu.VMEM((count, width, lev), jnp.float32),
            pltpu.VMEM((count, width, lev), jnp.float32),
            pltpu.VMEM((count, CHUNK + 16, lev), jnp.float32),
            pltpu.VMEM((width + 8, lev), jnp.float32),
        ],
        compiler_params=pltpu.CompilerParams(vmem_limit_bytes=VMEM_BYTES),
        cost_estimate=pl.CostEstimate(
            flops=20 * tracers.size, bytes_accessed=8 * tracers.size, transcendentals=0
        ),
        name="advect_rows",
    )(face, inverse, tracers, courants, prior, following, west, east, north, zonal)


def per_device(tendencies, bands, winds, tracers):
    lat_rows, width = tendencies.shape[1:3]
    lat_devices, lon_devices = lax.axis_size("lat"), lax.axis_size("lon")
    lat_count, lon_count = lat_devices * lat_rows, lon_devices * width
    half = lat_count // 2

    lat_on = [(i, i + 1) for i in range(lat_devices - 1)]
    lat_back = [(i + 1, i) for i in range(lat_devices - 1)]
    lon_on = [(i, (i + 1) % lon_devices) for i in range(lon_devices)]
    lon_back = [((i + 1) % lon_devices, i) for i in range(lon_devices)]

    def passed(block, axis, pairs):
        return lax.ppermute(block.astype(jnp.bfloat16), axis, pairs).astype(jnp.float32)

    own_ids = lax.axis_index("lat") * lat_rows + jnp.arange(lat_rows, dtype=jnp.int32)
    damping = 0.25 + 0.5 * (own_ids.astype(jnp.float32) + 0.5) / (lat_count / 2.0)
    keep = jnp.where(own_ids < half, damping, 1.0)
    near, far, send, shifts = filter_tables(
        2 * jnp.take(bands, own_ids) + 1, 1.0 - keep, lon_count, width
    )

    sent = project(tendencies, send)
    received, offset = [], 0
    for shift, rank in shifts:
        pairs = [
            (lat * lon_devices + i, lat * lon_devices + (i + shift) % lon_devices)
            for lat in range(lat_devices)
            if lat * lat_rows < half
            for i in range(lon_devices)
        ]
        piece = sent[:, offset : offset + 2 * rank]
        received.append(lax.ppermute(piece, ("lat", "lon"), pairs))
        offset += 2 * rank

    prior = passed(tracers[:, -1:], "lat", lat_on)
    following = passed(tracers[:, :1], "lat", lat_back)
    west = passed(tracers[:, :, -1:], "lon", lon_on)
    east = passed(tracers[:, :, :1], "lon", lon_back)

    filtered, courants = filter_rows(
        keep, tendencies, near, far, jnp.concatenate(received, axis=1), winds
    )
    north = passed(courants[1, 0], "lat", lat_back)
    zonal = passed(courants[0, :, :1], "lon", lon_back)

    centre_cos, _ = latitude_factors(own_ids, lat_count)
    first = lax.axis_index("lat") * lat_rows
    _, face_cos = latitude_factors(
        first + jnp.arange(lat_rows + 1, dtype=jnp.int32), lat_count
    )
    advected = advect(
        face_cos, 1.0 / centre_cos, tracers, courants, prior, following, west, east, north, zonal
    )
    return (filtered, advected)


def solution(mesh):
    spec = P(None, "lat", "lon", None)
    return jax.shard_map(
        per_device,
        mesh=mesh,
        in_specs=(spec, P(), spec, spec),
        out_specs=(spec, spec),
        check_vma=False,
    )
```

time: 908 us -> 119 us (0.13)
  the two profiles are of different devices: /device:TPU:0 before, /device:TPU:1 now
where the time goes in v1:
time: 119 us; the launch traced here: 118 us
  Pallas kernels  46 us (39%)
  starting transfers between devices  38.6 us (32%)
  other arithmetic  20.3 us (17%)
  waiting for transfers between devices  7.75 us (7%)
  local copies, waits for them, and re-layouts  3.91 us (3%)
    ppermute x7, starting transfers between devices, per_device(): received.append(lax.ppermute(piece, ('lat', 'lon'), pairs))  23.6 us
    pallas_call x1, Pallas kernels, advect(): pl.pallas_call(advect_kernel, grid=(rows + 1,), in_specs=[pl.BlockSpec(me...  19.8 us
    pallas_call x1, Pallas kernels, filter_rows(): pl.pallas_call(filter_kernel, grid=(rows,), in_specs=[pl.BlockSpec(memory...  16.6 us
    ppermute x6, starting transfers between devices, passed(): lax.ppermute(block.astype(jnp.bfloat16), axis, pairs).astype(jnp.float32)  14.9 us
    another operation x2, other arithmetic  12.3 us
    pallas_call x1, Pallas kernels, project(): pl.pallas_call(project_kernel, grid=(rows,), in_specs=[pl.BlockSpec((fiel...  9.62 us
    ppermute x7, waiting for transfers between devices, per_device(): received.append(lax.ppermute(piece, ('lat', 'lon'), pairs))  4.78 us
    convert_element_type x1, other arithmetic, filter_tables(): near = (near * strength[:, None, None]).astype(jnp.bfloat16)  4.07 us
  transfers between devices with their start and end apart: 13, of which 2 were waited for; matrix products, arithmetic and copies ran while one was open for 18% of the time, Pallas kernels for 14%

profile of v1, /device:TPU:1, one launch (start us, length us, event | category | flops | bytes accessed | tf_op | source)
XLA Modules:
  0.0 117.6 jit_solution(10637675372252095215)
XLA Ops:
  0.7 0.6 copy-done
  1.3 0.7 gather_fusion
  2.0 0.2 fusion.5
  2.2 1.2 %multiply_convert_fusion.2.send_ref = bf16[16,88,360]{2,1,0:T(8,128)(2,1)S(1)} fusion(f32[88,360]{1,0:T(8,128)} %constant.95.clone, f32[16,360]{1,0:T(8,128)S(1)} %get-tuple-element.21, f32[16,360]{1,0:T(8,128)S(1)} %get-tuple-element.22, pred[88]{0:T(512)(128)(4,1)} %constant.97), kind=kLoop, calls=%fused_computation.3 | loop fusion | flops 1520640 | bytes 1186648 | tf_op jit(solution)/shard_map/convert_element_type | solution.py:70
  3.4 9.6 %project_tendencies.1 = bf16[16,88,384]{2,1,0:T(8,128)(2,1)S(1)} custom-call(bf16[3,16,360,128]{3,2,1,0:T(8,128)(2,1)} %x_ref.3, bf16[16,88,360]{2,1,0:T(8,128)(2,1)S(1)} %multiply_convert_fusion.2.send_ref), custom_call_target="tpu_custom_call" | custom-call | flops 389283840 | bytes 5437440 | tf_op jit(solution)/shard_map/project_tendencies/pallas_call | solution.py:82
  13.1 6.1 %collective-permute-start.5 = (bf16[16,8,384]{2,1,0:T(8,128)(2,1)S(1)}, bf16[16,8,384]{2,1,0:T(8,128)(2,1)S(1)}, u32[]{:S(2)}, u32[]{:S(2)}) collective-permute-start(bf16[16,8,384]{2,1,0:T(8,128)(2,1)S(1)} %get-tuple-element.14), channel_id=1, source_target_pairs={{0,6},{1,7},{2,0},{3,1},{4,2},{5,3},{6,4},{7,5},{8,14},{9,15},{10,... | collective-permute-start | bytes 294920 | tf_op jit(solution)/shard_map/ppermute | solution.py:280
  19.1 2.0 %collective-permute-start.4 = (bf16[16,8,384]{2,1,0:T(8,128)(2,1)S(1)}, bf16[16,8,384]{2,1,0:T(8,128)(2,1)S(1)}, u32[]{:S(2)}, u32[]{:S(2)}) collective-permute-start(bf16[16,8,384]{2,1,0:T(8,128)(2,1)S(1)} %get-tuple-element.15), channel_id=1, source_target_pairs={{0,5},{1,6},{2,7},{3,0},{4,1},{5,2},{6,3},{7,4},{8,13},{9,14},{10,... | collective-permute-start | bytes 294920 | tf_op jit(solution)/shard_map/ppermute | solution.py:280
  21.2 5.1 %collective-permute-start.3 = (bf16[16,8,384]{2,1,0:T(8,128)(2,1)S(1)}, bf16[16,8,384]{2,1,0:T(8,128)(2,1)S(1)}, u32[]{:S(2)}, u32[]{:S(2)}) collective-permute-start(bf16[16,8,384]{2,1,0:T(8,128)(2,1)S(1)} %get-tuple-element.16), channel_id=1, source_target_pairs={{0,4},{1,5},{2,6},{3,7},{4,0},{5,1},{6,2},{7,3},{8,12},{9,13},{10,... | collective-permute-start | bytes 294920 | tf_op jit(solution)/shard_map/ppermute | solution.py:280
  26.3 1.9 %collective-permute-start.2 = (bf16[16,8,384]{2,1,0:T(8,128)(2,1)S(1)}, bf16[16,8,384]{2,1,0:T(8,128)(2,1)S(1)}, u32[]{:S(2)}, u32[]{:S(2)}) collective-permute-start(bf16[16,8,384]{2,1,0:T(8,128)(2,1)S(1)} %get-tuple-element.17), channel_id=1, source_target_pairs={{0,3},{1,4},{2,5},{3,6},{4,7},{5,0},{6,1},{7,2},{8,11},{9,12},{10,... | collective-permute-start | bytes 294920 | tf_op jit(solution)/shard_map/ppermute | solution.py:280
  28.2 0.1 fusion.19
  28.3 3.1 %collective-permute-start = (bf16[16,24,384]{2,1,0:T(8,128)(2,1)S(1)}, bf16[16,24,384]{2,1,0:T(8,128)(2,1)S(1)}, u32[]{:S(2)}, u32[]{:S(2)}) collective-permute-start(bf16[16,24,384]{2,1,0:T(8,128)(2,1)S(1)} %get-tuple-element.13), channel_id=1, source_target_pairs={{0,1},{1,2},{2,3},{3,4},{4,5},{5,6},{6,7},{7,0},{8,9},{9,10},{10,1... | collective-permute-start | bytes 884744 | tf_op jit(solution)/shard_map/ppermute | solution.py:280
  31.5 9.3 %convert.10 = bf16[5,16,360,128]{3,2,1,0:T(8,128)(2,1)} convert(f32[5,16,360,128]{3,2,1,0:T(8,128)} %tracer_ref.1) | non-fusion elementwise | flops 3686400 | bytes 22118400 | tf_op jit(solution)/shard_map/convert.5
  40.8 1.1 fusion.17
  41.9 1.2 %fusion.18 = (bf16[5,1,360,128]{3,2,1,0:T(8,128)(2,1)S(1)}, bf16[5,1,360,128]{3,2,1,0:T(8,128)(2,1)S(1)}) fusion(bf16[5,16,360,128]{3,2,1,0:T(8,128)(2,1)} %convert.10), kind=kLoop, calls=%fused_computation.47 | loop fusion | bytes 1843200 | tf_op jit(solution)/shard_map/slice | solution.py:284
  43.1 0.1 fusion.14
  43.3 4.1 %multiply_convert_fusion.near_ref = bf16[16,360,360]{2,1,0:T(8,128)(2,1)} fusion(f32[16]{0:T(128)S(1)} %broadcast_subtract_fusion, f32[16]{0:T(128)S(1)} %get-tuple-element.6, f32[360,360]{1,0:T(8,128)S(1)} %fusion, f32[360,360]{1,0:T(8,128)S(1)} %copy-done.2, f32[16,360]{1,0:T(8,128)S(1)} %get-tuple-element.22, f32[16,360]{1,0:T(8,128)S(1)} %get-tuple-element.21), kind=kLoop, calls=%fused_computation.1 | loop fusion | flops 16588800 | bytes 5230208 | tf_op jit(solution)/shard_map/convert_element_type | solution.py:59
  47.4 2.0 %multiply_convert_fusion.1.far_ref = bf16[16,360,88]{2,1,0:T(8,128)(2,1)S(1)} fusion(f32[16]{0:T(128)S(1)} %broadcast_subtract_fusion, f32[360,88]{1,0:T(8,128)S(1)} %copy-done.3, f32[16,88]{1,0:T(8,128)S(1)} %get-tuple-element.20, f32[16,360]{1,0:T(8,128)S(1)} %get-tuple-element.21, f32[16,88]{1,0:T(8,128)S(1)} %get-tuple-element.19, ...), kind=kLoop, calls=%fused_computation.2 | loop fusion | flops 3041280 | bytes 1197888 | tf_op jit(solution)/shard_map/convert_element_type | solution.py:68
  49.3 2.3 %collective-permute-start.1 = (bf16[16,8,384]{2,1,0:T(8,128)(2,1)S(1)}, bf16[16,8,384]{2,1,0:T(8,128)(2,1)S(1)}, u32[]{:S(2)}, u32[]{:S(2)}) collective-permute-start(bf16[16,8,384]{2,1,0:T(8,128)(2,1)S(1)} %get-tuple-element.18), channel_id=1, source_target_pairs={{0,2},{1,3},{2,4},{3,5},{4,6},{5,7},{6,0},{7,1},{8,10},{9,11},{10,... | collective-permute-start | bytes 294920 | tf_op jit(solution)/shard_map/ppermute | solution.py:280
  51.7 4.8 %collective-permute-done.1 = bf16[16,8,384]{2,1,0:T(8,128)(2,1)S(1)} collective-permute-done((bf16[16,8,384]{2,1,0:T(8,128)(2,1)S(1)}, bf16[16,8,384]{2,1,0:T(8,128)(2,1)S(1)}, u32[]{:S(2)}, u32[]{:S(2)}) %collective-permute-start.1) | collective-permute-done | bytes 98336 | tf_op jit(solution)/shard_map/ppermute | solution.py:280
  56.5 3.1 %collective-permute-start.6 = (bf16[16,24,384]{2,1,0:T(8,128)(2,1)S(1)}, bf16[16,24,384]{2,1,0:T(8,128)(2,1)S(1)}, u32[]{:S(2)}, u32[]{:S(2)}) collective-permute-start(bf16[16,24,384]{2,1,0:T(8,128)(2,1)S(1)} %get-tuple-element.12), channel_id=1, source_target_pairs={{0,7},{1,0},{2,1},{3,2},{4,3},{5,4},{6,5},{7,6},{8,15},{9,8},{10,9... | collective-permute-start | bytes 884744 | tf_op jit(solution)/shard_map/ppermute | solution.py:280
  59.6 0.3 collective-permute-start.10
  60.0 1.2 %collective-permute-start.9 = (bf16[5,16,1,128]{3,2,1,0:T(2,128)(2,1)S(1)}, bf16[5,16,1,128]{3,2,1,0:T(2,128)(2,1)S(1)}, u32[]{:S(2)}, u32[]{:S(2)}) collective-permute-start(bf16[5,16,1,128]{3,2,1,0:T(2,128)(2,1)S(1)} %get-tuple-element.9), channel_id=1, source_target_pairs={{0,1},{1,2},{2,3},{3,4},{4,5},{5,6},{6,7},{7,0},{8,9},{9,10},{10,1... | collective-permute-start | bytes 61448 | tf_op jit(solution)/shard_map/ppermute | solution.py:261
  61.3 5.7 %collective-permute-start.8 = (bf16[5,1,360,128]{3,2,1,0:T(8,128)(2,1)S(1)}, bf16[5,1,360,128]{3,2,1,0:T(8,128)(2,1)S(1)}, u32[]{:S(2)}, u32[]{:S(2)}) collective-permute-start(bf16[5,1,360,128]{3,2,1,0:T(8,128)(2,1)S(1)} %get-tuple-element.10), channel_id=1, source_target_pairs={{8,0},{16,8},{24,16},{9,1},{17,9},{25,17},{10,2},{18,10},{26,18},{... | collective-permute-start | bytes 1382408 | tf_op jit(solution)/shard_map/ppermute | solution.py:261
  67.0 1.9 %collective-permute-start.7 = (bf16[5,1,360,128]{3,2,1,0:T(8,128)(2,1)S(1)}, bf16[5,1,360,128]{3,2,1,0:T(8,128)(2,1)S(1)}, u32[]{:S(2)}, u32[]{:S(2)}) collective-permute-start(bf16[5,1,360,128]{3,2,1,0:T(8,128)(2,1)S(1)} %get-tuple-element.11), channel_id=1, source_target_pairs={{0,8},{8,16},{16,24},{1,9},{9,17},{17,25},{2,10},{10,18},{18,26},{... | collective-permute-start | bytes 1382408 | tf_op jit(solution)/shard_map/ppermute | solution.py:261
  69.0 16.6 %filter_rows.1 = (bf16[3,16,360,128]{3,2,1,0:T(8,128)(2,1)}, f32[2,16,360,128]{3,2,1,0:T(8,128)}) custom-call(f32[16]{0:T(128)S(1)} %compare_select_fusion.2.keep_ref, bf16[3,16,360,128]{3,2,1,0:T(8,128)(2,1)} %x_ref.3, bf16[16,360,360]{2,1,0:T(8,128)(2,1)} %multiply_convert_fusion.near_ref, bf16[16,360,88]{2,1,0:T(8,128)(2,1)S(1)} %multiply_convert_fusion.1.far_ref, ...), custom_call_target="tpu_custom_call" | custom-call | flops 1981808640 | bytes 20643840 | tf_op jit(solution)/shard_map/filter_rows/pallas_call | solution.py:119
  85.6 3.1 %convert.11 = bf16[2,16,360,128]{3,2,1,0:T(8,128)(2,1)S(1)} convert(f32[2,16,360,128]{3,2,1,0:T(8,128)} %get-tuple-element.5.courant_ref) | non-fusion elementwise | flops 1474560 | bytes 8847360 | tf_op jit(solution)/shard_map/convert.1
  88.7 3.0 %collective-permute-start.12 = (bf16[16,1,128]{2,1,0:T(2,128)(2,1)S(1)}, bf16[16,1,128]{2,1,0:T(2,128)(2,1)S(1)}, u32[]{:S(2)}, u32[]{:S(2)}) collective-permute-start(bf16[16,1,128]{2,1,0:T(2,128)(2,1)S(1)} %slice_bitcast_fusion.1), channel_id=1, source_target_pairs={{1,0},{2,1},{3,2},{4,3},{5,4},{6,5},{7,6},{0,7},{9,8},{10,9},{11,1... | collective-permute-start | bytes 12296 | tf_op jit(solution)/shard_map/ppermute | solution.py:261
  91.7 2.7 %collective-permute-start.11 = (bf16[360,128]{1,0:T(8,128)(2,1)S(1)}, bf16[360,128]{1,0:T(8,128)(2,1)S(1)}, u32[]{:S(2)}, u32[]{:S(2)}) collective-permute-start(bf16[360,128]{1,0:T(8,128)(2,1)S(1)} %slice_bitcast_fusion), channel_id=1, source_target_pairs={{8,0},{16,8},{24,16},{9,1},{17,9},{25,17},{10,2},{18,10},{26,18},{... | collective-permute-start | bytes 276488 | tf_op jit(solution)/shard_map/ppermute | solution.py:261
  94.6 3.0 %collective-permute-done.11 = bf16[360,128]{1,0:T(8,128)(2,1)S(1)} collective-permute-done((bf16[360,128]{1,0:T(8,128)(2,1)S(1)}, bf16[360,128]{1,0:T(8,128)(2,1)S(1)}, u32[]{:S(2)}, u32[]{:S(2)}) %collective-permute-start.11) | collective-permute-done | bytes 92192 | tf_op jit(solution)/shard_map/ppermute | solution.py:261
  97.6 0.1 convert_element_type.109.next_ref
  97.7 0.1 convert_element_type.108.prior_ref
  97.8 19.8 %advect_rows.1 = f32[5,16,360,128]{3,2,1,0:T(8,128)} custom-call(f32[17]{0:T(128)S(1)} %multiply_sine_fusion.face_ref, f32[16]{0:T(128)S(1)} %sine_divide_fusion.inverse_ref, f32[5,16,360,128]{3,2,1,0:T(8,128)} %tracer_ref.1, f32[2,16,360,128]{3,2,1,0:T(8,128)} %get-tuple-element.5.courant_ref, f32[5,1,360,128]{3,2,1,0:T(8,128)S(1)} %convert_element_type.108.prior_ref, ...), custom_call_target="tpu_custom_call" | custom-call | flops 73728000 | bytes 29491200 | tf_op jit(solution)/shard_map/advect_rows/pallas_call | solution.py:218
  (44 shorter events, 0.6 us)
Async XLA Ops:
  0.6 0.7 copy-start
  13.1 53.9 %collective-permute-start.5 = (bf16[16,8,384]{2,1,0:T(8,128)(2,1)S(1)}, bf16[16,8,384]{2,1,0:T(8,128)(2,1)S(1)}, u32[]{:S(2)}, u32[]{:S(2)}) collective-permute-start(bf16[16,8,384]{2,1,0:T(8,128)(2,1)S(1)} %get-tuple-element.14), channel_id=1, source_target_pairs={{0,6},{1,7},{2,0},{3,1},{4,2},{5,3},{6,4},{7,5},{8,14},{9,15},{10,... | collective-permute-start | bytes 294920 | tf_op jit(solution)/shard_map/ppermute | solution.py:280
  19.1 42.1 %collective-permute-start.4 = (bf16[16,8,384]{2,1,0:T(8,128)(2,1)S(1)}, bf16[16,8,384]{2,1,0:T(8,128)(2,1)S(1)}, u32[]{:S(2)}, u32[]{:S(2)}) collective-permute-start(bf16[16,8,384]{2,1,0:T(8,128)(2,1)S(1)} %get-tuple-element.15), channel_id=1, source_target_pairs={{0,5},{1,6},{2,7},{3,0},{4,1},{5,2},{6,3},{7,4},{8,13},{9,14},{10,... | collective-permute-start | bytes 294920 | tf_op jit(solution)/shard_map/ppermute | solution.py:280
  21.2 38.8 %collective-permute-start.3 = (bf16[16,8,384]{2,1,0:T(8,128)(2,1)S(1)}, bf16[16,8,384]{2,1,0:T(8,128)(2,1)S(1)}, u32[]{:S(2)}, u32[]{:S(2)}) collective-permute-start(bf16[16,8,384]{2,1,0:T(8,128)(2,1)S(1)} %get-tuple-element.16), channel_id=1, source_target_pairs={{0,4},{1,5},{2,6},{3,7},{4,0},{5,1},{6,2},{7,3},{8,12},{9,13},{10,... | collective-permute-start | bytes 294920 | tf_op jit(solution)/shard_map/ppermute | solution.py:280
  26.3 33.3 %collective-permute-start.2 = (bf16[16,8,384]{2,1,0:T(8,128)(2,1)S(1)}, bf16[16,8,384]{2,1,0:T(8,128)(2,1)S(1)}, u32[]{:S(2)}, u32[]{:S(2)}) collective-permute-start(bf16[16,8,384]{2,1,0:T(8,128)(2,1)S(1)} %get-tuple-element.17), channel_id=1, source_target_pairs={{0,3},{1,4},{2,5},{3,6},{4,7},{5,0},{6,1},{7,2},{8,11},{9,12},{10,... | collective-permute-start | bytes 294920 | tf_op jit(solution)/shard_map/ppermute | solution.py:280
  28.3 21.1 %collective-permute-start = (bf16[16,24,384]{2,1,0:T(8,128)(2,1)S(1)}, bf16[16,24,384]{2,1,0:T(8,128)(2,1)S(1)}, u32[]{:S(2)}, u32[]{:S(2)}) collective-permute-start(bf16[16,24,384]{2,1,0:T(8,128)(2,1)S(1)} %get-tuple-element.13), channel_id=1, source_target_pairs={{0,1},{1,2},{2,3},{3,4},{4,5},{5,6},{6,7},{7,0},{8,9},{9,10},{10,1... | collective-permute-start | bytes 884744 | tf_op jit(solution)/shard_map/ppermute | solution.py:280
  31.5 11.6 %copy-start.4 = (f32[88]{0:T(128)S(1)}, f32[88]{0:T(128)}, u32[]{:S(2)}) copy-start(f32[88]{0:T(128)} %constant.96) | copy-start | bytes 1060
  31.5 11.6 %copy-start.5 = (s32[88]{0:T(128)S(1)}, s32[88]{0:T(128)}, u32[]{:S(2)}) copy-start(s32[88]{0:T(128)} %constant.91.clone) | copy-start | bytes 1060
  31.5 11.8 %copy-start.2 = (f32[360,360]{1,0:T(8,128)S(1)}, f32[360,360]{1,0:T(8,128)}, u32[]{:S(2)}) copy-start(f32[360,360]{1,0:T(8,128)} %constant.90.clone) | copy-start | bytes 1555204
  43.1 4.2 %copy-start.3 = (f32[360,88]{1,0:T(8,128)S(1)}, f32[360,88]{1,0:T(8,128)}, u32[]{:S(2)}) copy-start(f32[360,88]{1,0:T(8,128)} %constant.93.clone) | copy-start | bytes 380164
  49.3 7.2 %collective-permute-start.1 = (bf16[16,8,384]{2,1,0:T(8,128)(2,1)S(1)}, bf16[16,8,384]{2,1,0:T(8,128)(2,1)S(1)}, u32[]{:S(2)}, u32[]{:S(2)}) collective-permute-start(bf16[16,8,384]{2,1,0:T(8,128)(2,1)S(1)} %get-tuple-element.18), channel_id=1, source_target_pairs={{0,2},{1,3},{2,4},{3,5},{4,6},{5,7},{6,0},{7,1},{8,10},{9,11},{10,... | collective-permute-start | bytes 294920 | tf_op jit(solution)/shard_map/ppermute | solution.py:280
  56.5 12.4 %collective-permute-start.6 = (bf16[16,24,384]{2,1,0:T(8,128)(2,1)S(1)}, bf16[16,24,384]{2,1,0:T(8,128)(2,1)S(1)}, u32[]{:S(2)}, u32[]{:S(2)}) collective-permute-start(bf16[16,24,384]{2,1,0:T(8,128)(2,1)S(1)} %get-tuple-element.12), channel_id=1, source_target_pairs={{0,7},{1,0},{2,1},{3,2},{4,3},{5,4},{6,5},{7,6},{8,15},{9,8},{10,9... | collective-permute-start | bytes 884744 | tf_op jit(solution)/shard_map/ppermute | solution.py:280
  59.6 32.1 %collective-permute-start.10 = (bf16[5,16,1,128]{3,2,1,0:T(2,128)(2,1)S(1)}, bf16[5,16,1,128]{3,2,1,0:T(2,128)(2,1)S(1)}, u32[]{:S(2)}, u32[]{:S(2)}) collective-permute-start(bf16[5,16,1,128]{3,2,1,0:T(2,128)(2,1)S(1)} %get-tuple-element.8), channel_id=1, source_target_pairs={{1,0},{2,1},{3,2},{4,3},{5,4},{6,5},{7,6},{0,7},{9,8},{10,9},{11,1... | collective-permute-start | bytes 61448 | tf_op jit(solution)/shard_map/ppermute | solution.py:261
  60.0 34.5 %collective-permute-start.9 = (bf16[5,16,1,128]{3,2,1,0:T(2,128)(2,1)S(1)}, bf16[5,16,1,128]{3,2,1,0:T(2,128)(2,1)S(1)}, u32[]{:S(2)}, u32[]{:S(2)}) collective-permute-start(bf16[5,16,1,128]{3,2,1,0:T(2,128)(2,1)S(1)} %get-tuple-element.9), channel_id=1, source_target_pairs={{0,1},{1,2},{2,3},{3,4},{4,5},{5,6},{6,7},{7,0},{8,9},{9,10},{10,1... | collective-permute-start | bytes 61448 | tf_op jit(solution)/shard_map/ppermute | solution.py:261
  61.3 36.3 %collective-permute-start.8 = (bf16[5,1,360,128]{3,2,1,0:T(8,128)(2,1)S(1)}, bf16[5,1,360,128]{3,2,1,0:T(8,128)(2,1)S(1)}, u32[]{:S(2)}, u32[]{:S(2)}) collective-permute-start(bf16[5,1,360,128]{3,2,1,0:T(8,128)(2,1)S(1)} %get-tuple-element.10), channel_id=1, source_target_pairs={{8,0},{16,8},{24,16},{9,1},{17,9},{25,17},{10,2},{18,10},{26,18},{... | collective-permute-start | bytes 1382408 | tf_op jit(solution)/shard_map/ppermute | solution.py:261
  67.0 30.7 %collective-permute-start.7 = (bf16[5,1,360,128]{3,2,1,0:T(8,128)(2,1)S(1)}, bf16[5,1,360,128]{3,2,1,0:T(8,128)(2,1)S(1)}, u32[]{:S(2)}, u32[]{:S(2)}) collective-permute-start(bf16[5,1,360,128]{3,2,1,0:T(8,128)(2,1)S(1)} %get-tuple-element.11), channel_id=1, source_target_pairs={{0,8},{8,16},{16,24},{1,9},{9,17},{17,25},{2,10},{10,18},{18,26},{... | collective-permute-start | bytes 1382408 | tf_op jit(solution)/shard_map/ppermute | solution.py:261
  88.7 5.9 %collective-permute-start.12 = (bf16[16,1,128]{2,1,0:T(2,128)(2,1)S(1)}, bf16[16,1,128]{2,1,0:T(2,128)(2,1)S(1)}, u32[]{:S(2)}, u32[]{:S(2)}) collective-permute-start(bf16[16,1,128]{2,1,0:T(2,128)(2,1)S(1)} %slice_bitcast_fusion.1), channel_id=1, source_target_pairs={{1,0},{2,1},{3,2},{4,3},{5,4},{6,5},{7,6},{0,7},{9,8},{10,9},{11,1... | collective-permute-start | bytes 12296 | tf_op jit(solution)/shard_map/ppermute | solution.py:261
  91.7 5.9 %collective-permute-start.11 = (bf16[360,128]{1,0:T(8,128)(2,1)S(1)}, bf16[360,128]{1,0:T(8,128)(2,1)S(1)}, u32[]{:S(2)}, u32[]{:S(2)}) collective-permute-start(bf16[360,128]{1,0:T(8,128)(2,1)S(1)} %slice_bitcast_fusion), channel_id=1, source_target_pairs={{8,0},{16,8},{24,16},{9,1},{17,9},{25,17},{10,2},{18,10},{26,18},{... | collective-permute-start | bytes 276488 | tf_op jit(solution)/shard_map/ppermute | solution.py:261
  97.8 19.9 %copy-start.1 = (s32[64]{0:T(128)S(1)}, s32[64]{0:T(128)}, u32[]{:S(2)}) copy-start(s32[64]{0:T(128)} %param.11) | copy-start | bytes 772

commit v2 on v1

v2 whole, which is shorter than its diff:
```python
import functools
import math

import jax
import jax.numpy as jnp
import numpy as np
from jax import lax
from jax.experimental import pallas as pl
from jax.experimental.pallas import tpu as pltpu
from jax.sharding import PartitionSpec as P

HEMI = 720
CHUNK = 24
VMEM_BYTES = 56 * 1024 * 1024
FACTOR_FLOOR = 1e-7


def latitude_factors(row_ids, lat_count):
    grid_row = row_ids.astype(jnp.float32) + jnp.float32(HEMI // 2 - lat_count // 2)
    centre_cos = jnp.sin(math.pi * (grid_row + 0.5) / (2.0 * HEMI))
    face_cos = jnp.sin(math.pi * grid_row / (2.0 * HEMI))
    return (centre_cos, face_cos)


@functools.lru_cache(maxsize=None)
def cosecant_factors(lon_count, width, group):
    cells = np.arange(width)
    apart = cells[:, None] - cells[None, :]
    safe = np.where(apart == 0, 1, apart)
    own = np.where(apart == 0, 0.0, 1.0 / (lon_count * np.sin(np.pi * safe / lon_count)))
    step = 8 // group
    targets, sources, offsets, is_sin, member, spans = [], [], [], [], [], []
    start = 0
    for shift in range(1, lon_count // width):
        block = 1.0 / (lon_count * np.sin(np.pi * (apart + shift * width) / lon_count))
        left, values, right = np.linalg.svd(block)
        rank = max(step, -(-int((values > FACTOR_FLOOR).sum()) // step) * step)
        root = np.sqrt(values[:rank])
        targets.append(np.tile(left[:, :rank] * root, (1, 2 * group)))
        sources.append(np.tile(root[:, None] * right[:rank], (2 * group, 1)))
        offsets.append(np.full(2 * group * rank, shift * width))
        is_sin.append(np.tile(np.repeat([False, True], rank), group))
        member.append(np.repeat(np.arange(group), 2 * rank))
        spans.append((shift, start, 2 * group * rank))
        start += 2 * group * rank
    return (
        own,
        np.concatenate(targets, 1),
        np.concatenate(sources, 0),
        np.concatenate(offsets),
        np.concatenate(is_sin),
        np.concatenate(member),
        tuple(spans),
    )


def filter_tables(odd, strength, lon_count, width, group):
    own, targets, sources, offsets, is_sin, member, spans = cosecant_factors(
        lon_count, width, group
    )

    def phase(cells):
        return (odd[:, None] * cells[None, :] % (2 * lon_count)).astype(jnp.float32) * (
            math.pi / lon_count
        )

    here = phase(jnp.arange(width, dtype=jnp.int32))
    sin_here, cos_here = jnp.sin(here), jnp.cos(here)
    near = (
        sin_here[:, :, None] * cos_here[:, None, :] - cos_here[:, :, None] * sin_here[:, None, :]
    ) * jnp.asarray(own, jnp.float32)
    near = near + jnp.eye(width, dtype=jnp.float32) * (odd.astype(jnp.float32) / lon_count)[
        :, None, None
    ]
    near = (near * strength[:, None, None]).astype(jnp.bfloat16)
    own_column = member[None, :] == np.arange(odd.shape[0])[:, None] % group
    moved = phase(jnp.asarray(offsets, jnp.int32)) - jnp.asarray(
        np.where(is_sin, math.pi / 2, 0.0), jnp.float32
    )
    weight = strength[:, None] * own_column
    far = (
        sin_here[:, :, None] * (weight * jnp.cos(moved))[:, None, :]
        + cos_here[:, :, None] * (weight * jnp.sin(moved))[:, None, :]
    )
    far = (far * jnp.asarray(targets, jnp.float32)).astype(jnp.bfloat16)
    use_sin = (own_column & is_sin).astype(np.float32)
    use_cos = (own_column & ~is_sin).astype(np.float32)
    send = use_sin[:, :, None] * sin_here[:, None, :] + use_cos[:, :, None] * cos_here[:, None, :]
    send = (send * jnp.asarray(sources, jnp.float32)).astype(jnp.bfloat16)
    return near, far, send, spans


def filter_kernel(
    spans, group, keep_ref, x_ref, send_ref, near_ref, far_ref, winds_ref, tracers_ref,
    filtered_ref, courant_ref, prior_ref, next_ref, west_ref, east_ref, north_ref, zonal_ref,
    winds, filtered, courants, total, outgoing, incoming, low_block, high_block, low, high, column,
    local_sem, send_sem, recv_sem, halo_send, halo_recv,
):
    fields, rows, width, lev = x_ref.shape
    tracer_count = tracers_ref.shape[0]
    lat, lon = lax.axis_index("lat"), lax.axis_index("lon")
    lat_devices, lon_devices = lax.axis_size("lat"), lax.axis_size("lon")
    has_prior, has_next = lat > 0, lat < lat_devices - 1
    lat_prior, lat_next = jnp.maximum(lat - 1, 0), jnp.minimum(lat + 1, lat_devices - 1)
    lon_west, lon_east = lax.rem(lon + lon_devices - 1, lon_devices), lax.rem(lon + 1, lon_devices)
    last_start = (width - 1) // 8 * 8

    winds_copy = pltpu.make_async_copy(winds_ref, winds, local_sem.at[0])
    low_copy = pltpu.make_async_copy(tracers_ref.at[:, :, pl.ds(0, 8)], low_block, local_sem.at[1])
    high_copy = pltpu.make_async_copy(
        tracers_ref.at[:, :, pl.ds(last_start, width - last_start)], high_block, local_sem.at[2]
    )
    low_copy.start()
    high_copy.start()
    winds_copy.start()

    barrier = pltpu.get_barrier_semaphore()
    for shift in range(1, lon_devices):
        pl.semaphore_signal(
            barrier, inc=1, device_id=(lat, lax.rem(lon + shift, lon_devices)),
            device_id_type=pl.DeviceIdType.MESH,
        )

    @pl.when(has_prior)
    def _():
        pl.semaphore_signal(
            barrier, inc=1, device_id=(lat_prior, lon), device_id_type=pl.DeviceIdType.MESH
        )

    @pl.when(has_next)
    def _():
        pl.semaphore_signal(
            barrier, inc=1, device_id=(lat_next, lon), device_id_type=pl.DeviceIdType.MESH
        )

    def field_row(j):
        return jnp.concatenate([x_ref[f, j] for f in range(fields)], axis=1)

    def project(p, carry):
        parts = [
            jnp.dot(send_ref[p * group + g], field_row(p * group + g), preferred_element_type=jnp.float32)
            for g in range(group)
        ]
        outgoing[p] = sum(parts[1:], parts[0]).astype(jnp.bfloat16)
        return carry

    lax.fori_loop(0, rows // group, project, 0)
    pl.semaphore_wait(barrier, lon_devices - 1 + has_prior.astype(jnp.int32) + has_next.astype(jnp.int32))

    def remote(source, target, sems, slot, device):
        return pltpu.make_async_remote_copy(
            src_ref=source, dst_ref=target, send_sem=sems[0].at[slot], recv_sem=sems[1].at[slot],
            device_id=device, device_id_type=pl.DeviceIdType.MESH,
        )

    exchanges = []
    for slot, (shift, start, size) in enumerate(spans):
        part = pl.ds(start, size)
        exchanges.append(
            remote(
                outgoing.at[:, part], incoming.at[:, part], (send_sem, recv_sem), slot,
                (lat, lax.rem(lon + shift, lon_devices)),
            )
        )
    for exchange in exchanges:
        exchange.start()

    halo = (halo_send, halo_recv)
    to_next = remote(tracers_ref.at[:, rows - 1], prior_ref, halo, 0, (lat_next, lon))
    to_prior = remote(tracers_ref.at[:, 0], next_ref, halo, 1, (lat_prior, lon))
    to_east = remote(high, west_ref, halo, 2, (lat, lon_east))
    to_west = remote(low, east_ref, halo, 3, (lat, lon_west))
    north_to_prior = remote(courants.at[1, 0], north_ref, halo, 4, (lat_prior, lon))
    zonal_to_west = remote(column, zonal_ref, halo, 5, (lat, lon_west))

    @pl.when(has_next)
    def _():
        to_next.start()

    @pl.when(has_prior)
    def _():
        to_prior.start()

    low_copy.wait()
    high_copy.wait()
    for q in range(tracer_count):
        for j in range(rows):
            low[q, j : j + 1, :] = low_block[q, j, 0:1, :]
            high[q, j : j + 1, :] = high_block[q, j, width - 1 - last_start : width - last_start, :]
    to_east.start()
    to_west.start()

    def near_row(j, carry):
        total[j] = jnp.dot(near_ref[j], field_row(j), preferred_element_type=jnp.float32)
        return carry

    lax.fori_loop(0, rows, near_row, 0)
    winds_copy.wait()
    for exchange in exchanges:
        exchange.wait_recv()

    def outputs(j):
        return (
            pltpu.make_async_copy(filtered.at[:, j], filtered_ref.at[:, j], local_sem.at[3]),
            pltpu.make_async_copy(courants.at[:, j], courant_ref.at[:, j], local_sem.at[4]),
        )

    def finish(j):
        far = jnp.dot(far_ref[j], incoming[j // group], preferred_element_type=jnp.float32)
        for f in range(fields):
            lanes = slice(f * lev, (f + 1) * lev)
            value = keep_ref[j] * x_ref[f, j].astype(jnp.float32) + total[j, :, lanes] + far[:, lanes]
            value = value.astype(jnp.bfloat16)
            filtered[f, j] = value
            if f < 2:
                courant = (0.5 if f == 0 else 0.25) * jnp.tanh(winds[f, j] + value.astype(jnp.float32))
                courants[f, j] = courant
                if f == 0:
                    column[pl.ds(j, 1), :] = courant[0:1, :]
        for copy in outputs(j):
            copy.start()

    finish(0)

    @pl.when(has_prior)
    def _():
        north_to_prior.start()

    def later(j, carry):
        finish(j)
        return carry

    lax.fori_loop(1, rows, later, 0)
    zonal_to_west.start()

    for exchange in exchanges:
        exchange.wait_send()
    to_east.wait()
    to_west.wait()
    zonal_to_west.wait()

    @pl.when(has_next)
    def _():
        to_next.wait_send()
        to_prior.wait_recv()
        north_to_prior.wait_recv()

    @pl.when(has_prior)
    def _():
        to_next.wait_recv()
        to_prior.wait_send()
        north_to_prior.wait_send()

    pltpu.make_async_copy(filtered, filtered_ref, local_sem.at[3]).wait()
    pltpu.make_async_copy(courants, courant_ref, local_sem.at[4]).wait()


def filter_rows(keep, tendencies, send, near, far, winds, tracers, spans, group):
    fields, rows, width, lev = tendencies.shape
    count = far.shape[2]
    tracer_count = tracers.shape[0]
    last = width - (width - 1) // 8 * 8
    hbm = pl.BlockSpec(memory_space=pl.ANY)
    vmem = pl.BlockSpec(memory_space=pltpu.VMEM)
    f32 = jnp.float32
    exchanged = (rows // group, count, fields * lev)
    return pl.pallas_call(
        functools.partial(filter_kernel, spans, group),
        in_specs=[pl.BlockSpec(memory_space=pltpu.SMEM), vmem, vmem, vmem, vmem, hbm, hbm],
        out_specs=[hbm] * 8,
        out_shape=[
            jax.ShapeDtypeStruct(tendencies.shape, jnp.bfloat16),
            jax.ShapeDtypeStruct(winds.shape, f32),
            jax.ShapeDtypeStruct((tracer_count, width, lev), f32),
            jax.ShapeDtypeStruct((tracer_count, width, lev), f32),
            jax.ShapeDtypeStruct((tracer_count, rows, lev), f32),
            jax.ShapeDtypeStruct((tracer_count, rows, lev), f32),
            jax.ShapeDtypeStruct((width, lev), f32),
            jax.ShapeDtypeStruct((rows, lev), f32),
        ],
        scratch_shapes=[
            pltpu.VMEM(winds.shape, f32),
            pltpu.VMEM(tendencies.shape, jnp.bfloat16),
            pltpu.VMEM(winds.shape, f32),
            pltpu.VMEM((rows, width, fields * lev), f32),
            pltpu.VMEM(exchanged, jnp.bfloat16),
            pltpu.VMEM(exchanged, jnp.bfloat16),
            pltpu.VMEM((tracer_count, rows, 8, lev), f32),
            pltpu.VMEM((tracer_count, rows, last, lev), f32),
            pltpu.VMEM((tracer_count, rows, lev), f32),
            pltpu.VMEM((tracer_count, rows, lev), f32),
            pltpu.VMEM((rows, lev), f32),
            pltpu.SemaphoreType.DMA((5,)),
            pltpu.SemaphoreType.DMA((len(spans),)),
            pltpu.SemaphoreType.DMA((len(spans),)),
            pltpu.SemaphoreType.DMA((6,)),
            pltpu.SemaphoreType.DMA((6,)),
        ],
        compiler_params=pltpu.CompilerParams(
            vmem_limit_bytes=VMEM_BYTES, collective_id=0, has_side_effects=True
        ),
        cost_estimate=pl.CostEstimate(
            flops=2 * rows * (width + 2 * count) * width * fields * lev,
            bytes_accessed=4 * tendencies.size + 8 * winds.size,
            transcendentals=winds.size,
        ),
        name="filter_rows",
    )(keep, tendencies, send, near, far, winds, tracers)


def advect_kernel(
    edges_ref, face_ref, inverse_ref, tracer_ref, courant_ref, passing_ref, prior_ref, next_ref,
    west_ref, east_ref, north_ref, zonal_ref, out_ref, passed_ref, before, partial, edge, shifted,
):
    tracers, _, width, _ = tracer_ref.shape
    step = pl.program_id(0)
    rows = pl.num_programs(0) - 1
    face = face_ref[step]
    inverse_before = inverse_ref[jnp.maximum(step - 1, 0)]
    chunks = [(start, min(CHUNK, width - start)) for start in range(0, width, CHUNK)]

    @pl.when(step == 0)
    def _():
        before[...] = jnp.where(edges_ref[0] > 0, prior_ref[...], 0.0)
        partial[...] = jnp.zeros_like(partial)

    @pl.when(step < rows)
    def _():
        inverse = inverse_ref[jnp.minimum(step, rows - 1)]
        passed_ref[...] = passing_ref[...]
        shifted[0:width, :] = courant_ref[0, 0]
        shifted[width : width + 1, :] = zonal_ref[pl.ds(step, 1), :]
        for start, size in chunks:
            part = pl.ds(start, size)
            here = courant_ref[0, 0, part, :]
            there = shifted[pl.ds(start + 1, size), :]
            north = courant_ref[1, 0, part, :]
            here_up, here_down = jnp.maximum(here, 0.0), jnp.minimum(here, 0.0)
            there_up, there_down = jnp.maximum(there, 0.0), jnp.minimum(there, 0.0)
            north_up = face * jnp.maximum(north, 0.0)
            north_down = face * jnp.minimum(north, 0.0)
            for q in range(tracers):
                value = tracer_ref[q, 0, part, :]
                if start == 0:
                    edge[q, 7:8, :] = west_ref[q, pl.ds(step, 1), :]
                    edge[q, pl.ds(8, size), :] = value
                    west = edge[q, pl.ds(7, size), :]
                else:
                    west = tracer_ref[q, 0, pl.ds(start - 1, size), :]
                if start + size == width:
                    edge[q, pl.ds(8, size), :] = value
                    edge[q, pl.ds(8 + size, 1), :] = east_ref[q, pl.ds(step, 1), :]
                    east = edge[q, pl.ds(9, size), :]
                else:
                    east = tracer_ref[q, 0, pl.ds(start + 1, size), :]
                flux = north_up * before[q, part, :] + north_down * value
                out_ref[q, 0, part, :] = partial[q, part, :] - flux * inverse_before
                zonal = (there_up * value + there_down * east) - (here_up * west + here_down * value)
                partial[q, part, :] = value - zonal + flux * inverse
                before[q, part, :] = value

    @pl.when(step == rows)
    def _():
        for start, size in chunks:
            part = pl.ds(start, size)
            north = jnp.where(edges_ref[1] > 0, north_ref[part, :], 0.0)
            north_up = face * jnp.maximum(north, 0.0)
            north_down = face * jnp.minimum(north, 0.0)
            for q in range(tracers):
                below = jnp.where(edges_ref[1] > 0, next_ref[q, part, :], 0.0)
                flux = north_up * before[q, part, :] + north_down * below
                out_ref[q, 0, part, :] = partial[q, part, :] - flux * inverse_before


def advect(edges, face, inverse, tracers, courants, filtered, halos):
    count, rows, width, lev = tracers.shape
    fields = filtered.shape[0]

    def clipped(j):
        return (0, jnp.minimum(j, rows - 1), 0, 0)

    smem = pl.BlockSpec(memory_space=pltpu.SMEM)
    vmem = pl.BlockSpec(memory_space=pltpu.VMEM)
    return pl.pallas_call(
        advect_kernel,
        grid=(rows + 1,),
        in_specs=[
            smem,
            smem,
            smem,
            pl.BlockSpec((count, 1, width, lev), clipped),
            pl.BlockSpec((2, 1, width, lev), clipped),
            pl.BlockSpec((fields, 1, width, lev), clipped),
        ]
        + [vmem] * len(halos),
        out_specs=[
            pl.BlockSpec((count, 1, width, lev), lambda j: (0, jnp.maximum(j - 1, 0), 0, 0)),
            pl.BlockSpec((fields, 1, width, lev), clipped),
        ],
        out_shape=[
            jax.ShapeDtypeStruct(tracers.shape, jnp.float32),
            jax.ShapeDtypeStruct(filtered.shape, filtered.dtype),
        ],
        scratch_shapes=[
            pltpu.VMEM((count, width, lev), jnp.float32),
            pltpu.VMEM((count, width, lev), jnp.float32),
            pltpu.VMEM((count, CHUNK + 16, lev), jnp.float32),
            pltpu.VMEM((width + 8, lev), jnp.float32),
        ],
        compiler_params=pltpu.CompilerParams(vmem_limit_bytes=VMEM_BYTES),
        cost_estimate=pl.CostEstimate(
            flops=20 * tracers.size, bytes_accessed=8 * tracers.size, transcendentals=0
        ),
        name="advect_rows",
    )(edges, face, inverse, tracers, courants, filtered, *halos)


def per_device(tendencies, bands, winds, tracers):
    lat_rows, width = tendencies.shape[1:3]
    lat_devices, lon_devices = lax.axis_size("lat"), lax.axis_size("lon")
    lat_count, lon_count = lat_devices * lat_rows, lon_devices * width
    place = lax.axis_index("lat")
    group = 2 - lat_rows % 2

    own_ids = place * lat_rows + jnp.arange(lat_rows, dtype=jnp.int32)
    damping = 0.25 + 0.5 * (own_ids.astype(jnp.float32) + 0.5) / (lat_count / 2.0)
    keep = jnp.where(own_ids < lat_count // 2, damping, 1.0)
    near, far, send, spans = filter_tables(
        2 * jnp.take(bands, own_ids) + 1, 1.0 - keep, lon_count, width, group
    )
    filtered, courants, *halos = filter_rows(
        keep, tendencies, send, near, far, winds, tracers, spans, group
    )
    centre_cos, _ = latitude_factors(own_ids, lat_count)
    _, face_cos = latitude_factors(
        place * lat_rows + jnp.arange(lat_rows + 1, dtype=jnp.int32), lat_count
    )
    edges = jnp.stack([place > 0, place < lat_devices - 1]).astype(jnp.int32)
    advected, filtered = advect(
        edges, face_cos, 1.0 / centre_cos, tracers, courants, filtered, halos
    )
    return (filtered, advected)


def solution(mesh):
    spec = P(None, "lat", "lon", None)
    return jax.shard_map(
        per_device,
        mesh=mesh,
        in_specs=(spec, P(), spec, spec),
        out_specs=(spec, spec),
        check_vma=False,
    )
```

time: 119 us -> 79 us (0.66)
  the two profiles are of different devices: /device:TPU:1 before, /device:TPU:10 now
where the time goes in v2:
time: 79 us; the launch traced here: 78.4 us
  Pallas kernels  62.4 us (79%)
  other arithmetic  14.6 us (18%)
    pallas_call x1, Pallas kernels, filter_rows(): pl.pallas_call(functools.partial(filter_kernel, spans, group), in_specs=[...  40.1 us
    pallas_call x1, Pallas kernels, advect(): pl.pallas_call(advect_kernel, grid=(rows + 1,), in_specs=[smem, smem, sme...  22.3 us
    convert_element_type x1, other arithmetic, filter_tables(): far = (far * jnp.asarray(targets, jnp.float32)).astype(jnp.bfloat16)  4.09 us
    convert_element_type x1, other arithmetic, filter_tables(): near = (near * strength[:, None, None]).astype(jnp.bfloat16)  4.03 us
    convert_element_type x1, other arithmetic, filter_tables(): send = (send * jnp.asarray(sources, jnp.float32)).astype(jnp.bfloat16)  2.94 us

profile of v2, /device:TPU:10, one launch (start us, length us, event | category | flops | bytes accessed | tf_op | source)
XLA Modules:
  0.0 78.4 jit_solution(12017714204520217590)
XLA Ops:
  0.6 0.0 copy-start
  0.6 0.0 copy-start.2
  0.7 0.6 add_convert_fusion.edges_ref
  1.3 0.6 multiply_sine_fusion.face_ref
  1.9 0.6 sine_divide_fusion
  2.6 0.0 copy-done
  2.6 0.7 gather_fusion
  3.2 0.5 convert_multiply_fusion
  3.8 0.9 %select_multiply_fusion.1 = (f32[16,176]{1,0:T(8,128)S(1)}, f32[16,176]{1,0:T(8,128)S(1)}) fusion(pred[16,176]{1,0:T(8,128)(4,1)} %constant.103.clone, f32[176]{0:T(256)} %constant.110, s32[176]{0:T(256)} %constant.101.clone, s32[16]{0:T(128)S(1)} %get-tuple-element.23, f32[16]{0:T(128)S(1)} %get-tuple-element.30), kind=kLoop, calls=%fused_computation.17 | loop fusion | flops 36608 | bytes 26880 | tf_op jit(solution)/shard_map/mul | solution.py:82
  4.6 0.2 fusion.6
  4.9 2.9 %multiply_convert_fusion.2.send_ref = bf16[16,176,360]{2,1,0:T(8,128)(2,1)} fusion(f32[176,360]{1,0:T(8,128)} %constant.107.clone, f32[16,360]{1,0:T(8,128)S(1)} %get-tuple-element.27, f32[16,176]{1,0:T(8,128)} %constant.109, f32[16,360]{1,0:T(8,128)S(1)} %get-tuple-element.26, f32[16,176]{1,0:T(8,128)} %constant.108), kind=kLoop, calls=%fused_computation.3 | loop fusion | flops 5068800 | bytes 2349568 | tf_op jit(solution)/shard_map/convert_element_type | solution.py:89
  7.8 4.1 %multiply_convert_fusion.1.far_ref = bf16[16,360,176]{2,1,0:T(8,128)(2,1)} fusion(f32[360,176]{1,0:T(8,128)} %constant.104.clone, f32[16,176]{1,0:T(8,128)S(1)} %get-tuple-element.25, f32[16,360]{1,0:T(8,128)S(1)} %get-tuple-element.27, f32[16,176]{1,0:T(8,128)S(1)} %get-tuple-element.24, f32[16,360]{1,0:T(8,128)S(1)} %get-tuple-element.26), kind=kLoop, calls=%fused_computation.2 | loop fusion | flops 5068800 | bytes 2349568 | tf_op jit(solution)/shard_map/convert_element_type | solution.py:85
  11.9 0.0 copy-done.2
  11.9 4.0 %multiply_convert_fusion.near_ref = bf16[16,360,360]{2,1,0:T(8,128)(2,1)} fusion(f32[16]{0:T(128)S(1)} %get-tuple-element.30, f32[16]{0:T(128)S(1)} %get-tuple-element.22, f32[360,360]{1,0:T(8,128)S(1)} %fusion, f32[360,360]{1,0:T(8,128)S(1)} %copy-done.2, f32[16,360]{1,0:T(8,128)S(1)} %get-tuple-element.26, f32[16,360]{1,0:T(8,128)S(1)} %get-tuple-element.27), kind=kLoop, calls=%fused_computation.1 | loop fusion | flops 16588800 | bytes 5230208 | tf_op jit(solution)/shard_map/convert_element_type | solution.py:75
  15.9 40.1 %filter_rows.1 = (bf16[3,16,360,128]{3,2,1,0:T(8,128)(2,1)}, f32[2,16,360,128]{3,2,1,0:T(8,128)}, f32[5,360,128]{2,1,0:T(8,128)}, f32[5,360,128]{2,1,0:T(8,128)}...) custom-call(f32[16]{0:T(128)} %get-tuple-element.28.keep_ref, ...), custom_call_target="tpu_custom_call" | custom-call | flops 3149660160 | bytes 20643840 | tf_op jit(solution)/shard_map/filter_rows/pallas_call | solution.py:267
  56.0 0.0 copy-start.1
  56.1 22.3 %advect_rows.1 = (f32[5,16,360,128]{3,2,1,0:T(8,128)}, bf16[3,16,360,128]{3,2,1,0:T(8,128)(2,1)}) custom-call(s32[2]{0:T(128)} %add_convert_fusion.edges_ref, f32[17]{0:T(128)} %multiply_sine_fusion.face_ref, f32[16]{0:T(128)} %get-tuple-element.29.inverse_ref, f32[5,16,360,128]{3,2,1,0:T(8,128)} %tracer_ref.1, ...), custom_call_target="tpu_custom_call" | custom-call | flops 73728000 | bytes 29491200 | tf_op jit(solution)/shard_map/advect_rows/pallas_call | solution.py:384
  78.4 0.0 copy-done.1
  (3 shorter events, 0.0 us)
Async XLA Ops:
  0.6 1.9 %copy-start = (s32[64]{0:T(128)S(1)}, s32[64]{0:T(128)}, u32[]{:S(2)}) copy-start(s32[64]{0:T(128)} %param.13) | copy-start | bytes 772
  0.6 11.3 %copy-start.2 = (f32[360,360]{1,0:T(8,128)S(1)}, f32[360,360]{1,0:T(8,128)}, u32[]{:S(2)}) copy-start(f32[360,360]{1,0:T(8,128)} %constant.100.clone) | copy-start | bytes 1555204
  56.0 22.3 %copy-start.1 = (s32[64]{0:T(128)S(1)}, s32[64]{0:T(128)}, u32[]{:S(2)}) copy-start(s32[64]{0:T(128)} %param.13) | copy-start | bytes 772

commit v3 on v2

--- a/solution.py
+++ b/solution.py
@@ -15,11 +15,14 @@
 FACTOR_FLOOR = 1e-7
 
 
-def latitude_factors(row_ids, lat_count):
-    grid_row = row_ids.astype(jnp.float32) + jnp.float32(HEMI // 2 - lat_count // 2)
-    centre_cos = jnp.sin(math.pi * (grid_row + 0.5) / (2.0 * HEMI))
-    face_cos = jnp.sin(math.pi * grid_row / (2.0 * HEMI))
-    return (centre_cos, face_cos)
+def latitude_factors(lat_count):
+    row = np.arange(lat_count + 1, dtype=np.float64)
+    grid_row = row + (HEMI // 2 - lat_count // 2)
+    inverse = 1.0 / np.sin(np.pi * (grid_row[:-1] + 0.5) / (2.0 * HEMI))
+    face_cos = np.sin(np.pi * grid_row / (2.0 * HEMI))
+    damping = 0.25 + 0.5 * (row[:-1] + 0.5) / (lat_count / 2.0)
+    keep = np.where(row[:-1] < lat_count // 2, damping, 1.0)
+    return [table.astype(np.float32) for table in (face_cos, inverse, keep)]
 
 
 @functools.lru_cache(maxsize=None)
@@ -29,7 +32,7 @@
     safe = np.where(apart == 0, 1, apart)
     own = np.where(apart == 0, 0.0, 1.0 / (lon_count * np.sin(np.pi * safe / lon_count)))
     step = 8 // group
-    targets, sources, offsets, is_sin, member, spans = [], [], [], [], [], []
+    targets, sources, part, member, spans = [], [], [], [], []
     start = 0
     for shift in range(1, lon_count // width):
         block = 1.0 / (lon_count * np.sin(np.pi * (apart + shift * width) / lon_count))
@@ -38,60 +41,35 @@
         root = np.sqrt(values[:rank])
         targets.append(np.tile(left[:, :rank] * root, (1, 2 * group)))
         sources.append(np.tile(root[:, None] * right[:rank], (2 * group, 1)))
-        offsets.append(np.full(2 * group * rank, shift * width))
-        is_sin.append(np.tile(np.repeat([False, True], rank), group))
+        part.append(np.tile(np.repeat([0, 1], rank), group))
         member.append(np.repeat(np.arange(group), 2 * rank))
         spans.append((shift, start, 2 * group * rank))
         start += 2 * group * rank
+    masks = np.stack(
+        [
+            (np.concatenate(member) == g) & (np.concatenate(part) == which)
+            for g in range(group)
+            for which in (0, 1)
+        ]
+    )
     return (
-        own,
-        np.concatenate(targets, 1),
-        np.concatenate(sources, 0),
-        np.concatenate(offsets),
-        np.concatenate(is_sin),
-        np.concatenate(member),
+        own.astype(np.float32),
+        (np.concatenate(targets, 1) * masks[:, None, :]).astype(np.float32),
+        (np.concatenate(sources, 0) * masks[:, :, None]).astype(np.float32),
         tuple(spans),
     )
 
 
-def filter_tables(odd, strength, lon_count, width, group):
-    own, targets, sources, offsets, is_sin, member, spans = cosecant_factors(
-        lon_count, width, group
-    )
-
-    def phase(cells):
-        return (odd[:, None] * cells[None, :] % (2 * lon_count)).astype(jnp.float32) * (
-            math.pi / lon_count
-        )
-
-    here = phase(jnp.arange(width, dtype=jnp.int32))
-    sin_here, cos_here = jnp.sin(here), jnp.cos(here)
-    near = (
-        sin_here[:, :, None] * cos_here[:, None, :] - cos_here[:, :, None] * sin_here[:, None, :]
-    ) * jnp.asarray(own, jnp.float32)
-    near = near + jnp.eye(width, dtype=jnp.float32) * (odd.astype(jnp.float32) / lon_count)[
-        :, None, None
-    ]
-    near = (near * strength[:, None, None]).astype(jnp.bfloat16)
-    own_column = member[None, :] == np.arange(odd.shape[0])[:, None] % group
-    moved = phase(jnp.asarray(offsets, jnp.int32)) - jnp.asarray(
-        np.where(is_sin, math.pi / 2, 0.0), jnp.float32
-    )
-    weight = strength[:, None] * own_column
-    far = (
-        sin_here[:, :, None] * (weight * jnp.cos(moved))[:, None, :]
-        + cos_here[:, :, None] * (weight * jnp.sin(moved))[:, None, :]
-    )
-    far = (far * jnp.asarray(targets, jnp.float32)).astype(jnp.bfloat16)
-    use_sin = (own_column & is_sin).astype(np.float32)
-    use_cos = (own_column & ~is_sin).astype(np.float32)
-    send = use_sin[:, :, None] * sin_here[:, None, :] + use_cos[:, :, None] * cos_here[:, None, :]
-    send = (send * jnp.asarray(sources, jnp.float32)).astype(jnp.bfloat16)
-    return near, far, send, spans
+def waves(odd, cells, lon_count):
+    phase = (odd[:, None] * cells[None, :] % (2 * lon_count)).astype(jnp.float32) * (
+        math.pi / lon_count
+    )
+    return jnp.sin(phase), jnp.cos(phase)
 
 
 def filter_kernel(
-    spans, group, keep_ref, x_ref, send_ref, near_ref, far_ref, winds_ref, tracers_ref,
+    spans, group, halves, keep_ref, own_ref, sin_shift, cos_shift, x_ref, sin_row, cos_row,
+    sin_column, cos_column, csc_ref, target_ref, source_ref, winds_ref, tracers_ref,
     filtered_ref, courant_ref, prior_ref, next_ref, west_ref, east_ref, north_ref, zonal_ref,
     winds, filtered, courants, total, outgoing, incoming, low_block, high_block, low, high, column,
     local_sem, send_sem, recv_sem, halo_send, halo_recv,
@@ -137,14 +115,26 @@
         return jnp.concatenate([x_ref[f, j] for f in range(fields)], axis=1)
 
     def project(p, carry):
-        parts = [
-            jnp.dot(send_ref[p * group + g], field_row(p * group + g), preferred_element_type=jnp.float32)
-            for g in range(group)
-        ]
+        parts = []
+        for g in range(group):
+            j = p * group + g
+            sines, cosines = sin_row[pl.ds(j, 1), :], cos_row[pl.ds(j, 1), :]
+            pieces = []
+            for slot, (_, start, size) in enumerate(spans):
+                sin_s, cos_s = sin_shift[j, slot], cos_shift[j, slot]
+                moved_cos = cosines * cos_s + sines * sin_s
+                moved_sin = sines * cos_s - cosines * sin_s
+                piece = slice(start, start + size)
+                pieces.append(
+                    source_ref[2 * g, piece, :] * moved_cos + source_ref[2 * g + 1, piece, :] * moved_sin
+                )
+            table = jnp.concatenate(pieces, axis=0).astype(jnp.bfloat16)
+            parts.append(jnp.dot(table, field_row(j), preferred_element_type=jnp.float32))
         outgoing[p] = sum(parts[1:], parts[0]).astype(jnp.bfloat16)
         return carry
 
-    lax.fori_loop(0, rows // group, project, 0)
+    groups = rows // group // halves
+    lax.fori_loop(0, groups, project, 0)
     pl.semaphore_wait(barrier, lon_devices - 1 + has_prior.astype(jnp.int32) + has_next.astype(jnp.int32))
 
     def remote(source, target, sems, slot, device):
@@ -153,17 +143,21 @@
             device_id=device, device_id_type=pl.DeviceIdType.MESH,
         )
 
-    exchanges = []
-    for slot, (shift, start, size) in enumerate(spans):
-        part = pl.ds(start, size)
-        exchanges.append(
-            remote(
-                outgoing.at[:, part], incoming.at[:, part], (send_sem, recv_sem), slot,
-                (lat, lax.rem(lon + shift, lon_devices)),
+    exchanges = [[] for _ in range(halves)]
+    for half in range(halves):
+        for slot, (shift, start, size) in enumerate(spans):
+            part = (pl.ds(half * groups, groups), pl.ds(start, size))
+            exchanges[half].append(
+                remote(
+                    outgoing.at[part], incoming.at[part], (send_sem, recv_sem),
+                    half * len(spans) + slot, (lat, lax.rem(lon + shift, lon_devices)),
+                )
             )
-        )
-    for exchange in exchanges:
-        exchange.start()
+    for half in range(halves):
+        if half > 0:
+            lax.fori_loop(half * groups, (half + 1) * groups, project, 0)
+        for exchange in exchanges[half]:
+            exchange.start()
 
     halo = (halo_send, halo_recv)
     to_next = remote(tracers_ref.at[:, rows - 1], prior_ref, halo, 0, (lat_next, lon))
@@ -190,14 +184,18 @@
     to_east.start()
     to_west.start()
 
+    def column_of(ref, j):
+        return pltpu.roll(ref[...], lax.rem(128 - j, 128), 1)[:, 0:1]
+
     def near_row(j, carry):
-        total[j] = jnp.dot(near_ref[j], field_row(j), preferred_element_type=jnp.float32)
+        sines, cosines = sin_row[pl.ds(j, 1), :], cos_row[pl.ds(j, 1), :]
+        own_sin, own_cos = column_of(sin_column, j), column_of(cos_column, j)
+        table = (own_sin * cosines - own_cos * sines) * csc_ref[...]
+        total[j] = jnp.dot(table.astype(jnp.bfloat16), field_row(j), preferred_element_type=jnp.float32)
         return carry
 
     lax.fori_loop(0, rows, near_row, 0)
     winds_copy.wait()
-    for exchange in exchanges:
-        exchange.wait_recv()
 
     def outputs(j):
         return (
@@ -205,11 +203,15 @@
             pltpu.make_async_copy(courants.at[:, j], courant_ref.at[:, j], local_sem.at[4]),
         )
 
-    def finish(j):
-        far = jnp.dot(far_ref[j], incoming[j // group], preferred_element_type=jnp.float32)
+    def finish(p, g):
+        j = p * group + g
+        own_sin, own_cos = column_of(sin_column, j), column_of(cos_column, j)
+        table = own_sin * target_ref[2 * g] - own_cos * target_ref[2 * g + 1]
+        far = jnp.dot(table.astype(jnp.bfloat16), incoming[p], preferred_element_type=jnp.float32)
+        keep = keep_ref[lat * rows + j] + own_ref[j]
         for f in range(fields):
             lanes = slice(f * lev, (f + 1) * lev)
-            value = keep_ref[j] * x_ref[f, j].astype(jnp.float32) + total[j, :, lanes] + far[:, lanes]
+            value = keep * x_ref[f, j].astype(jnp.float32) + total[j, :, lanes] + far[:, lanes]
             value = value.astype(jnp.bfloat16)
             filtered[f, j] = value
             if f < 2:
@@ -220,20 +222,27 @@
         for copy in outputs(j):
             copy.start()
 
-    finish(0)
-
-    @pl.when(has_prior)
-    def _():
-        north_to_prior.start()
-
-    def later(j, carry):
-        finish(j)
+    def later(p, carry):
+        for g in range(group):
+            finish(p, g)
         return carry
 
-    lax.fori_loop(1, rows, later, 0)
+    for half in range(halves):
+        for exchange in exchanges[half]:
+            exchange.wait_recv()
+        first = half * groups
+        if half == 0:
+            later(0, 0)
+
+            @pl.when(has_prior)
+            def _():
+                north_to_prior.start()
+
+            first = 1
+        lax.fori_loop(first, (half + 1) * groups, later, 0)
     zonal_to_west.start()
 
-    for exchange in exchanges:
+    for exchange in sum(exchanges, []):
         exchange.wait_send()
     to_east.wait()
     to_west.wait()
@@ -255,9 +264,10 @@
     pltpu.make_async_copy(courants, courant_ref, local_sem.at[4]).wait()
 
 
-def filter_rows(keep, tendencies, send, near, far, winds, tracers, spans, group):
+def filter_rows(scalars, tendencies, tables, winds, tracers, spans, group):
     fields, rows, width, lev = tendencies.shape
-    count = far.shape[2]
+    count = tables[-1].shape[1]
+    halves = 2 - rows // group % 2
     tracer_count = tracers.shape[0]
     last = width - (width - 1) // 8 * 8
     hbm = pl.BlockSpec(memory_space=pl.ANY)
@@ -265,8 +275,10 @@
     f32 = jnp.float32
     exchanged = (rows // group, count, fields * lev)
     return pl.pallas_call(
-        functools.partial(filter_kernel, spans, group),
-        in_specs=[pl.BlockSpec(memory_space=pltpu.SMEM), vmem, vmem, vmem, vmem, hbm, hbm],
+        functools.partial(filter_kernel, spans, group, halves),
+        in_specs=[pl.BlockSpec(memory_space=pltpu.SMEM)] * len(scalars)
+        + [vmem] * (1 + len(tables))
+        + [hbm, hbm],
         out_specs=[hbm] * 8,
         out_shape=[
             jax.ShapeDtypeStruct(tendencies.shape, jnp.bfloat16),
@@ -291,8 +303,8 @@
             pltpu.VMEM((tracer_count, rows, lev), f32),
             pltpu.VMEM((rows, lev), f32),
             pltpu.SemaphoreType.DMA((5,)),
-            pltpu.SemaphoreType.DMA((len(spans),)),
-            pltpu.SemaphoreType.DMA((len(spans),)),
+            pltpu.SemaphoreType.DMA((halves * len(spans),)),
+            pltpu.SemaphoreType.DMA((halves * len(spans),)),
             pltpu.SemaphoreType.DMA((6,)),
             pltpu.SemaphoreType.DMA((6,)),
         ],
@@ -305,28 +317,30 @@
             transcendentals=winds.size,
         ),
         name="filter_rows",
-    )(keep, tendencies, send, near, far, winds, tracers)
+    )(*scalars, tendencies, *tables, winds, tracers)
 
 
 def advect_kernel(
-    edges_ref, face_ref, inverse_ref, tracer_ref, courant_ref, passing_ref, prior_ref, next_ref,
+    face_ref, inverse_ref, tracer_ref, courant_ref, passing_ref, prior_ref, next_ref,
     west_ref, east_ref, north_ref, zonal_ref, out_ref, passed_ref, before, partial, edge, shifted,
 ):
     tracers, _, width, _ = tracer_ref.shape
     step = pl.program_id(0)
     rows = pl.num_programs(0) - 1
-    face = face_ref[step]
-    inverse_before = inverse_ref[jnp.maximum(step - 1, 0)]
+    lat = lax.axis_index("lat")
+    has_prior, has_next = lat > 0, lat < lax.axis_size("lat") - 1
+    face = face_ref[lat * rows + step]
+    inverse_before = inverse_ref[lat * rows + jnp.maximum(step - 1, 0)]
     chunks = [(start, min(CHUNK, width - start)) for start in range(0, width, CHUNK)]
 
     @pl.when(step == 0)
     def _():
-        before[...] = jnp.where(edges_ref[0] > 0, prior_ref[...], 0.0)
+        before[...] = jnp.where(has_prior, prior_ref[...], 0.0)
         partial[...] = jnp.zeros_like(partial)
 
     @pl.when(step < rows)
     def _():
-        inverse = inverse_ref[jnp.minimum(step, rows - 1)]
+        inverse = inverse_ref[lat * rows + step]
         passed_ref[...] = passing_ref[...]
         shifted[0:width, :] = courant_ref[0, 0]
         shifted[width : width + 1, :] = zonal_ref[pl.ds(step, 1), :]
@@ -363,16 +377,16 @@
     def _():
         for start, size in chunks:
             part = pl.ds(start, size)
-            north = jnp.where(edges_ref[1] > 0, north_ref[part, :], 0.0)
+            north = jnp.where(has_next, north_ref[part, :], 0.0)
             north_up = face * jnp.maximum(north, 0.0)
             north_down = face * jnp.minimum(north, 0.0)
             for q in range(tracers):
-                below = jnp.where(edges_ref[1] > 0, next_ref[q, part, :], 0.0)
+                below = jnp.where(has_next, next_ref[q, part, :], 0.0)
                 flux = north_up * before[q, part, :] + north_down * below
                 out_ref[q, 0, part, :] = partial[q, part, :] - flux * inverse_before
 
 
-def advect(edges, face, inverse, tracers, courants, filtered, halos):
+def advect(face, inverse, tracers, courants, filtered, halos):
     count, rows, width, lev = tracers.shape
     fields = filtered.shape[0]
 
@@ -385,7 +399,6 @@
         advect_kernel,
         grid=(rows + 1,),
         in_specs=[
-            smem,
             smem,
             smem,
             pl.BlockSpec((count, 1, width, lev), clipped),
@@ -412,7 +425,7 @@
             flops=20 * tracers.size, bytes_accessed=8 * tracers.size, transcendentals=0
         ),
         name="advect_rows",
-    )(edges, face, inverse, tracers, courants, filtered, *halos)
+    )(face, inverse, tracers, courants, filtered, *halos)
 
 
 def per_device(tendencies, bands, winds, tracers):
@@ -422,22 +435,26 @@
     place = lax.axis_index("lat")
     group = 2 - lat_rows % 2
 
-    own_ids = place * lat_rows + jnp.arange(lat_rows, dtype=jnp.int32)
-    damping = 0.25 + 0.5 * (own_ids.astype(jnp.float32) + 0.5) / (lat_count / 2.0)
-    keep = jnp.where(own_ids < lat_count // 2, damping, 1.0)
-    near, far, send, spans = filter_tables(
-        2 * jnp.take(bands, own_ids) + 1, 1.0 - keep, lon_count, width, group
-    )
+    face_cos, inverse, keep = latitude_factors(lat_count)
+    csc, targets, sources, spans = cosecant_factors(lon_count, width, group)
+    odd = 2 * lax.dynamic_slice_in_dim(bands, place * lat_rows, lat_rows) + 1
+    strength = 1.0 - lax.dynamic_slice_in_dim(jnp.asarray(keep), place * lat_rows, lat_rows)
+    sin_row, cos_row = waves(odd, jnp.arange(width, dtype=jnp.int32), lon_count)
+    shifts = np.array([shift * width for shift, _, _ in spans], np.int32)
+    sin_shift, cos_shift = waves(odd, jnp.asarray(shifts), lon_count)
+    columns = [
+        jnp.pad((table * strength[:, None]).T, ((0, 0), (0, 128 - lat_rows)))
+        for table in (sin_row, cos_row)
+    ]
+    own = strength * odd.astype(jnp.float32) / lon_count
     filtered, courants, *halos = filter_rows(
-        keep, tendencies, send, near, far, winds, tracers, spans, group
-    )
-    centre_cos, _ = latitude_factors(own_ids, lat_count)
-    _, face_cos = latitude_factors(
-        place * lat_rows + jnp.arange(lat_rows + 1, dtype=jnp.int32), lat_count
-    )
-    edges = jnp.stack([place > 0, place < lat_devices - 1]).astype(jnp.int32)
+        (jnp.asarray(keep), own, sin_shift, cos_shift),
+        tendencies,
+        (sin_row, cos_row, *columns, jnp.asarray(csc), jnp.asarray(targets), jnp.asarray(sources)),
+        winds, tracers, spans, group,
+    )
     advected, filtered = advect(
-        edges, face_cos, 1.0 / centre_cos, tracers, courants, filtered, halos
+        jnp.asarray(face_cos), jnp.asarray(inverse), tracers, courants, filtered, halos
     )
     return (filtered, advected)
 

time: 79 us -> 66.3 us (0.84)
  the two profiles are of different devices: /device:TPU:10 before, /device:TPU:0 now
where the time goes in v3:
time: 66.3 us; the launch traced here: 65.7 us
  Pallas kernels  59.3 us (89%)
  other arithmetic  4.28 us (6%)
  local copies, waits for them, and re-layouts  1.49 us (2%)
    pallas_call x1, Pallas kernels, filter_rows(): pl.pallas_call(functools.partial(filter_kernel, spans, group, halves), in...  36.9 us
    pallas_call x1, Pallas kernels, advect(): pl.pallas_call(advect_kernel, grid=(rows + 1,), in_specs=[smem, smem, pl....  22.4 us
    cos x2, other arithmetic, waves(): return (jnp.sin(phase), jnp.cos(phase))  2.19 us
    pad x2, local copies, waits for them, and re-layouts, per_device(): jnp.pad((table * strength[:, None]).T, ((0, 0), (0, 128 - lat_rows)))  1.38 us
    div x1, other arithmetic, per_device(): own = strength * odd.astype(jnp.float32) / lon_count  1.34 us

profile of v3, /device:TPU:0, one launch (start us, length us, event | category | flops | bytes accessed | tf_op | source)
XLA Modules:
  0.0 65.7 jit_solution(4085367702182275947)
XLA Ops:
  0.6 1.3 %multiply_multiply_fusion = (f32[16]{0:T(128)}, s32[16]{0:T(128)S(1)}, f32[16]{0:T(128)S(1)}) fusion(f32[64]{0:T(128)} %constant.56.clone.keep_ref, s32[]{:T(128)S(6)} %select_n.21, s32[64]{0:T(128)} %param.12), kind=kLoop, calls=%fused_computation.26 | loop fusion | flops 96 | bytes 324 | tf_op jit(solution)/shard_map/div | solution.py:449
  2.0 1.4 %fusion.15 = (f32[16,7]{1,0:T(8,128)}, f32[16,7]{1,0:T(8,128)}) fusion(s32[7]{0:T(128)} %constant.57.clone, s32[16]{0:T(128)S(1)} %get-tuple-element.23), kind=kLoop, calls=%fused_computation.23 | loop fusion | flops 1008 | bytes 988 | tf_op jit(solution)/shard_map/cos | solution.py:67
  3.4 0.1 fusion.2
  3.4 0.8 %fusion.7 = (f32[16,360]{1,0:T(8,128)}, f32[16,360]{1,0:T(8,128)}) fusion(s32[16]{0:T(128)S(1)} %get-tuple-element.23), kind=kLoop, calls=%fused_computation.13 | loop fusion | flops 51840 | bytes 46144 | tf_op jit(solution)/shard_map/cos | solution.py:67
  4.3 0.1 copy.13
  4.4 0.7 %cosine_multiply_fusion = (f32[360,16]{1,0:T(8,128)S(1)}, f32[360,16]{1,0:T(8,128)S(1)}) fusion(f32[360,16]{1,0:T(8,128)S(1)} %copy.13, f32[16]{0:T(128)S(1)} %get-tuple-element.28), kind=kLoop, calls=%fused_computation | loop fusion | flops 17280 | bytes 69184 | tf_op jit(solution)/shard_map/mul | solution.py:446
  5.1 0.7 %pad.8.cos_column = f32[360,128]{1,0:T(8,128)} pad(f32[360,16]{1,0:T(8,128)S(1)} %get-tuple-element.24, f32[]{:T(128)} %constant.55.clone.1), padding=0_0x0_112 | pad | bytes 207364 | tf_op jit(solution)/shard_map/jit(_pad)/pad | solution.py:446
  5.7 0.7 %pad.7.sin_column = f32[360,128]{1,0:T(8,128)} pad(f32[360,16]{1,0:T(8,128)S(1)} %get-tuple-element.25, f32[]{:T(128)} %constant.55.clone.1), padding=0_0x0_112 | pad | bytes 207364 | tf_op jit(solution)/shard_map/jit(_pad)/pad | solution.py:446
  6.4 36.9 %filter_rows.1 = (bf16[3,16,360,128]{3,2,1,0:T(8,128)(2,1)}, f32[2,16,360,128]{3,2,1,0:T(8,128)}, f32[5,360,128]{2,1,0:T(8,128)}, f32[5,360,128]{2,1,0:T(8,128)}...) custom-call(f32[64]{0:T(128)} %constant.56.clone.keep_ref, ...), custom_call_target="tpu_custom_call" | custom-call | flops 3149660160 | bytes 20643840 | tf_op jit(solution)/shard_map/filter_rows/pallas_call | solution.py:277
  43.3 22.4 %advect_rows.1 = (f32[5,16,360,128]{3,2,1,0:T(8,128)}, bf16[3,16,360,128]{3,2,1,0:T(8,128)(2,1)}) custom-call(f32[65]{0:T(128)} %constant.61.clone.face_ref, f32[64]{0:T(128)} %constant.62.clone.inverse_ref, f32[5,16,360,128]{3,2,1,0:T(8,128)} %tracer_ref.1, f32[2,16,360,128]{3,2,1,0:T(8,128)} %get-tuple-element.12.courant_ref, ...), custom_call_target="tpu_custom_call" | custom-call | flops 73728000 | bytes 29491200 | tf_op jit(solution)/shard_map/advect_rows/pallas_call | solution.py:398

commit v4 on v3

--- a/solution.py
+++ b/solution.py
@@ -353,6 +353,10 @@
             there_up, there_down = jnp.maximum(there, 0.0), jnp.minimum(there, 0.0)
             north_up = face * jnp.maximum(north, 0.0)
             north_down = face * jnp.minimum(north, 0.0)
+            before_share = north_up * inverse
+            value_share = (1.0 - there_up + here_down) + north_down * inverse
+            before_taken = north_up * inverse_before
+            value_taken = north_down * inverse_before
             for q in range(tracers):
                 value = tracer_ref[q, 0, part, :]
                 if start == 0:
@@ -367,10 +371,11 @@
                     east = edge[q, pl.ds(9, size), :]
                 else:
                     east = tracer_ref[q, 0, pl.ds(start + 1, size), :]
-                flux = north_up * before[q, part, :] + north_down * value
-                out_ref[q, 0, part, :] = partial[q, part, :] - flux * inverse_before
-                zonal = (there_up * value + there_down * east) - (here_up * west + here_down * value)
-                partial[q, part, :] = value - zonal + flux * inverse
+                prior = before[q, part, :]
+                out_ref[q, 0, part, :] = partial[q, part, :] - before_taken * prior - value_taken * value
+                partial[q, part, :] = (
+                    value_share * value + before_share * prior + here_up * west - there_down * east
+                )
                 before[q, part, :] = value
 
     @pl.when(step == rows)
@@ -442,10 +447,12 @@
     sin_row, cos_row = waves(odd, jnp.arange(width, dtype=jnp.int32), lon_count)
     shifts = np.array([shift * width for shift, _, _ in spans], np.int32)
     sin_shift, cos_shift = waves(odd, jnp.asarray(shifts), lon_count)
-    columns = [
-        jnp.pad((table * strength[:, None]).T, ((0, 0), (0, 128 - lat_rows)))
-        for table in (sin_row, cos_row)
-    ]
+    spare = (0, 128 - lat_rows)
+    column_phase = (
+        jnp.arange(width, dtype=jnp.int32)[:, None] * jnp.pad(odd, spare)[None, :] % (2 * lon_count)
+    ).astype(jnp.float32) * (math.pi / lon_count)
+    column_scale = jnp.pad(strength, spare)[None, :]
+    columns = [jnp.sin(column_phase) * column_scale, jnp.cos(column_phase) * column_scale]
     own = strength * odd.astype(jnp.float32) / lon_count
     filtered, courants, *halos = filter_rows(
         (jnp.asarray(keep), own, sin_shift, cos_shift),

time: 66.3 us -> 64.8 us (0.977)
  local copies, waits for them, and re-layouts: 1.49 us -> 0.01 us
  Pallas kernels: 59.3 us -> 58.5 us
  other arithmetic: 4.28 us -> 5.06 us
    pad x2, local copies, waits for them, and re-layouts: 1.38 us -> 0.01 us  [the longest x1 0.01 us: per_device(): column_scale = jnp.pad(strength, spare)[None, :]]
    mul x1, other arithmetic: 0.67 us -> 1.53 us  [per_device(): jnp.cos(column_phase) * column_scale]
    pallas_call x1, Pallas kernels: 22.4 us -> 21.6 us  [advect(): pl.pallas_call(advect_kernel, grid=(rows + 1,), in_specs=[smem, smem, pl....]
where the time goes in v4:
time: 64.8 us; the launch traced here: 64.2 us
  Pallas kernels  58.5 us (90%)
  other arithmetic  5.06 us (8%)
  between operations  0.65 us (1%)
    pallas_call x1, Pallas kernels, filter_rows(): pl.pallas_call(functools.partial(filter_kernel, spans, group, halves), in...  36.9 us
    pallas_call x1, Pallas kernels, advect(): pl.pallas_call(advect_kernel, grid=(rows + 1,), in_specs=[smem, smem, pl....  21.6 us
    cos x2, other arithmetic, waves(): return (jnp.sin(phase), jnp.cos(phase))  2.2 us
    mul x1, other arithmetic, per_device(): jnp.cos(column_phase) * column_scale  1.53 us
    div x1, other arithmetic, per_device(): own = strength * odd.astype(jnp.float32) / lon_count  1.34 us

profile of v4, /device:TPU:0, one launch (start us, length us, event | category | flops | bytes accessed | tf_op | source)
XLA Modules:
  0.0 64.2 jit_solution(5893938255000603879)
XLA Ops:
  0.6 1.3 %multiply_multiply_fusion = (f32[16]{0:T(128)}, s32[16]{0:T(128)S(1)}, f32[16]{0:T(128)S(1)}) fusion(f32[64]{0:T(128)} %constant.63.clone.keep_ref, s32[]{:T(128)S(6)} %select_n.23, s32[64]{0:T(128)} %param.12), kind=kLoop, calls=%fused_computation.27 | loop fusion | flops 96 | bytes 324 | tf_op jit(solution)/shard_map/div | solution.py:456
  2.0 1.4 %fusion.16 = (f32[16,7]{1,0:T(8,128)}, f32[16,7]{1,0:T(8,128)}) fusion(s32[7]{0:T(128)} %constant.64.clone, s32[16]{0:T(128)S(1)} %get-tuple-element.23), kind=kLoop, calls=%fused_computation.24 | loop fusion | flops 1008 | bytes 988 | tf_op jit(solution)/shard_map/cos | solution.py:67
  3.4 0.8 %fusion.9 = (f32[16,360]{1,0:T(8,128)}, f32[16,360]{1,0:T(8,128)}) fusion(s32[16]{0:T(128)S(1)} %get-tuple-element.23), kind=kLoop, calls=%fused_computation.15 | loop fusion | flops 51840 | bytes 46144 | tf_op jit(solution)/shard_map/cos | solution.py:67
  4.2 1.5 %cosine_multiply_fusion = (f32[360,128]{1,0:T(8,128)}, f32[360,128]{1,0:T(8,128)}) fusion(f32[128]{0:T(128)S(1)} %pad.9, s32[128]{0:T(128)S(1)} %pad.8), kind=kLoop, calls=%fused_computation.3 | loop fusion | flops 506880 | bytes 369664 | tf_op jit(solution)/shard_map/mul | solution.py:455
  5.7 36.9 %filter_rows.1 = (bf16[3,16,360,128]{3,2,1,0:T(8,128)(2,1)}, f32[2,16,360,128]{3,2,1,0:T(8,128)}, f32[5,360,128]{2,1,0:T(8,128)}, f32[5,360,128]{2,1,0:T(8,128)}...) custom-call(f32[64]{0:T(128)} %constant.63.clone.keep_ref, ...), custom_call_target="tpu_custom_call" | custom-call | flops 3149660160 | bytes 20643840 | tf_op jit(solution)/shard_map/filter_rows/pallas_call | solution.py:277
  42.6 21.6 %advect_rows.1 = (f32[5,16,360,128]{3,2,1,0:T(8,128)}, bf16[3,16,360,128]{3,2,1,0:T(8,128)(2,1)}) custom-call(f32[65]{0:T(128)} %constant.68.clone.face_ref, f32[64]{0:T(128)} %constant.69.clone.inverse_ref, f32[5,16,360,128]{3,2,1,0:T(8,128)} %tracer_ref.1, f32[2,16,360,128]{3,2,1,0:T(8,128)} %get-tuple-element.12.courant_ref, ...), custom_call_target="tpu_custom_call" | custom-call | flops 73728000 | bytes 29491200 | tf_op jit(solution)/shard_map/advect_rows/pallas_call | solution.py:403
  (2 shorter events, 0.0 us)
